TPU v7x, 512 devices: a whole 4x8x8 slice. The times are simulated.
512 devices in a mesh: tm: 64 (over x, z, core), rows: 8 (over y).
Axes of the slice: x: 4, y: 8, z: 8, core: 2. Of those that a mesh axis runs over, the one named last changes fastest.
Arguments:
- observations: float32 [128, 64, 1024], P('tm', 'rows'), may hold values from -6 to 6
- obs_noise: float32 [128, 64, 1024], P('tm', 'rows'), may hold values from -6 to 6
- prior_noise: float32 [128, 64, 1024], P('tm', 'rows'), may hold values from -4.8 to 4.8
- observed: int32 [128, 64, 1024], P('tm', 'rows'), may hold values 0 or 1
- kappa_sq: float32 [64, 1024], P('rows'), may hold values from 0.5 to 8
- obs_precision: float32 [64, 1024], P('rows'), may hold values from 0.2 to 2
Outputs:
- solution: float32 [128, 64, 1024], P('tm', 'rows')
- residual: float32 [128, 64, 1024], P('tm', 'rows')
- precond: float32 [128, 64, 1024], P('tm', 'rows')
All inputs are finite; a program needn't handle non-finite values. No bound on the sum of `observed` on one device may be relied on, other than what follows from the above.
Results may differ from a plain program's by a relative error of at most 0.002.
Values sent between devices are 32-bit elements; how exact they have to be, the bound alone decides.
A program may use at most 64 MiB of HBM per device.

v0:
```python
import jax
import jax.numpy as jnp
from jax import lax
from jax.sharding import PartitionSpec as P

ITERS = 2


coupling = 0.995


def with_halo(array, sides, width):
    for axis, dim in sides:
        devices, length = (lax.axis_size(axis), array.shape[dim])
        up = [(i, (i + 1) % devices) for i in range(devices - 1)]
        down = [(j, i) for i, j in up]
        last = lax.slice_in_dim(array, length - width, length, axis=dim)
        initial = lax.slice_in_dim(array, 0, width, axis=dim)
        before = lax.ppermute(last, axis, up)
        after = lax.ppermute(initial, axis, down)
        array = jnp.concatenate([before, array, after], axis=dim)
    return array


def carried_in(value, axis, join, neutral, backward):
    count, mine = (lax.axis_size(axis), lax.axis_index(axis))
    pieces = jax.tree.map(lambda part: lax.all_gather(part, axis), value)
    if backward:
        pieces = jax.tree.map(lambda part: part[::-1], pieces)
        mine = count - 1 - mine
    so_far = jax.tree.map(
        lambda part, zero: jnp.full_like(part, 0) + jnp.asarray(zero, part.dtype), value, neutral
    )

    def turn(position, so_far):
        longer = join(so_far, jax.tree.map(lambda part: part[position], pieces))
        return jax.tree.map(lambda new, old: jnp.where(position < mine, new, old), longer, so_far)

    return lax.fori_loop(0, count - 1, turn, so_far)


def mat_combine(earlier, later):
    e_upper_left, e_upper_right, e_lower_left, e_lower_right = earlier
    l_upper_left, l_upper_right, l_lower_left, l_lower_right = later
    new_ul = l_upper_left * e_upper_left + l_upper_right * e_lower_left
    new_ur = l_upper_left * e_upper_right + l_upper_right * e_lower_right
    new_ll = l_lower_left * e_upper_left + l_lower_right * e_lower_left
    new_lr = l_lower_left * e_upper_right + l_lower_right * e_lower_right
    largest = jnp.maximum(
        jnp.maximum(jnp.abs(new_ul), jnp.abs(new_ur)), jnp.maximum(jnp.abs(new_ll), jnp.abs(new_lr))
    )
    return (new_ul / largest, new_ur / largest, new_ll / largest, new_lr / largest)


def affine_combine(earlier, later):
    return (later[0] * earlier[0], later[0] * earlier[1] + later[1])


def local_product(main_diagonal_entries, offdiagonal_entries):
    unit_field = jnp.ones_like(offdiagonal_entries)
    empty_field_grid = jnp.zeros_like(offdiagonal_entries)

    def local_advance(current_state, main_row):
        factor_now = (empty_field_grid, offdiagonal_entries, -offdiagonal_entries, main_row)
        return (mat_combine(current_state, factor_now), None)

    state_end, unused_item = lax.scan(
        local_advance,
        (unit_field, empty_field_grid, empty_field_grid, unit_field),
        main_diagonal_entries,
        reverse=False,
    )
    return state_end


def pivots(main_diagonal_entries, offdiagonal_entries, ratio_start):

    def pivots_advance(previous_ratio, main_row):
        pivot_entry = main_row - offdiagonal_entries * previous_ratio
        current_ratio = offdiagonal_entries / pivot_entry
        return (current_ratio, (previous_ratio, pivot_entry, current_ratio))

    unused_item, (ratio_before, pivot_rows, ratio_rows) = lax.scan(
        pivots_advance, ratio_start, main_diagonal_entries, reverse=False
    )
    return (ratio_before, pivot_rows, ratio_rows)


def apply_affine_scan(decay_rate, source, backward):

    def apply_advance(value_prev, matrix_entries):
        rate_row, forcing_row = matrix_entries
        current_value = rate_row * value_prev + forcing_row
        return (current_value, current_value)

    unused_item, value_list = lax.scan(
        apply_advance, jnp.zeros_like(source[0]), (decay_rate, source), reverse=backward
    )
    return value_list


def reverse_cumprod(value_list):
    return jnp.flip(jnp.cumprod(jnp.flip(value_list, 0), axis=0), 0)


def operate(field, stencil_diag, weights, obs_weight):
    padded = with_halo(field, (("rows", 1),), 1)
    column_zero = jnp.zeros_like(field[:, :, :1])
    left_part = jnp.concatenate([column_zero, field[:, :, :-1]], axis=2)
    right_side = jnp.concatenate([field[:, :, 1:], column_zero], axis=2)
    beside = padded[:, 2:] + padded[:, :-2] + right_side + left_part
    spatial = stencil_diag * field - beside
    hour_pad = with_halo(spatial, (("tm", 0),), 1)
    return weights * spatial - coupling * (hour_pad[2:] + hour_pad[:-2]) + obs_weight * field


def inner_total(value_list):
    return lax.psum(jnp.sum(value_list), ("tm", "rows"))


def curve_total(value_list):
    return lax.psum(jnp.sum(value_list), ("tm", "rows"))


def per_device(observations, obs_noise, prior_noise, observed, kappa_sq, obs_precision):
    hour_block = observations.shape[0]
    maskf = observed.astype(jnp.float32)
    obs_weight = maskf * obs_precision
    right = (
        maskf * (obs_precision * observations + jnp.sqrt(obs_precision) * obs_noise) + prior_noise
    )
    stencil_diag = kappa_sq + 4.0
    hour_count = hour_block * lax.axis_size("tm")
    global_hour = lax.axis_index("tm") * hour_block + jnp.arange(hour_block, dtype=jnp.int32)
    boundary = (global_hour == 0) | (global_hour == hour_count - 1)
    weights = jnp.where(boundary, 1.0, 1.0 + coupling * coupling).astype(jnp.float32)[:, None, None]
    main_diagonal_entries = weights * stencil_diag + obs_weight
    offdiagonal_entries = -coupling * stencil_diag
    unit_field = jnp.ones_like(offdiagonal_entries)
    empty_field_grid = jnp.zeros_like(offdiagonal_entries)
    identity_mat = (unit_field, empty_field_grid, empty_field_grid, unit_field)
    front_pair = carried_in(
        local_product(main_diagonal_entries, offdiagonal_entries),
        "tm",
        mat_combine,
        identity_mat,
        False,
    )
    ratio_start = front_pair[1] / front_pair[3]
    ratio_before, pivot_rows, ratio_rows = pivots(
        main_diagonal_entries, offdiagonal_entries, ratio_start
    )
    decay_rate = -offdiagonal_entries / pivot_rows
    rate_cum = jnp.cumprod(decay_rate, axis=0)

    def forward_solve(right_hand_part):
        partial_result = apply_affine_scan(decay_rate, right_hand_part / pivot_rows, False)
        incoming = carried_in(
            (rate_cum[-1], partial_result[-1]),
            "tm",
            affine_combine,
            (unit_field, empty_field_grid),
            False,
        )
        return (partial_result + rate_cum * incoming[1], incoming[1])

    sweep_factor = -ratio_rows
    cum_sweep = reverse_cumprod(sweep_factor)

    def solve(right_hand_part):
        leading_elimination, unused_item = forward_solve(right_hand_part)
        partial_result = apply_affine_scan(sweep_factor, leading_elimination, True)
        incoming = carried_in(
            (cum_sweep[0], partial_result[0]),
            "tm",
            affine_combine,
            (unit_field, empty_field_grid),
            True,
        )
        return partial_result + cum_sweep * incoming[1]

    solution = jnp.zeros_like(right)
    residual = right
    precond = solve(residual)
    direction = precond
    aligned = inner_total(residual * precond)
    for iteration in range(ITERS):
        applied = operate(direction, stencil_diag, weights, obs_weight)
        step_size = aligned / curve_total(direction * applied)
        solution = solution + step_size * direction
        residual = residual - step_size * applied
        precond = solve(residual)
        aligned_new = inner_total(residual * precond)
        direction = precond + aligned_new / aligned * direction
        aligned = aligned_new
    return (solution, residual, precond)


def solution(mesh):
    in_specs = (
        P("tm", "rows", None),
        P("tm", "rows", None),
        P("tm", "rows", None),
        P("tm", "rows", None),
        P("rows", None),
        P("rows", None),
    )
    out_specs = (P("tm", "rows", None), P("tm", "rows", None), P("tm", "rows", None))
    return jax.shard_map(
        per_device, mesh=mesh, in_specs=in_specs, out_specs=out_specs, check_vma=False
    )
```

profile of v0, /device:TPU:1, one launch (start us, length us, event | category | flops | bytes accessed | tf_op | source)
XLA Modules:
  0.0 1664.1 jit_solution(7104511991550490368)
XLA Ops:
  12.0 89.3 %all-gather.33.cloned.1.call-done = f32[512,1024]{1,0:T(8,128)} async-done(((f32[8,1024]{1,0:T(8,128)}), f32[512,1024]{1,0:T(8,128)}) %all-gather.33.cloned.1.call-update) | async-done | bytes 2097168 | tf_op jit(solution)/shard_map/all_gather | solution.py:27
  101.2 84.6 %all-gather.35.cloned.1.call-done = f32[512,1024]{1,0:T(8,128)} async-done(((f32[8,1024]{1,0:T(8,128)}), f32[512,1024]{1,0:T(8,128)}) %all-gather.35.cloned.1.call-update) | async-done | bytes 2097168 | tf_op jit(solution)/shard_map/all_gather | solution.py:27
  185.8 84.6 %all-gather.37.cloned.1.call-done = f32[512,1024]{1,0:T(8,128)} async-done(((f32[8,1024]{1,0:T(8,128)}), f32[512,1024]{1,0:T(8,128)}) %all-gather.37.cloned.1.call-update) | async-done | bytes 2097168 | tf_op jit(solution)/shard_map/all_gather | solution.py:27
  270.4 83.9 %all-gather.39.cloned.1.call-done = f32[512,1024]{1,0:T(8,128)} async-done(((f32[8,1024]{1,0:T(8,128)}), f32[512,1024]{1,0:T(8,128)}) %all-gather.39.cloned.1.call-update) | async-done | bytes 2097168 | tf_op jit(solution)/shard_map/all_gather | solution.py:27
  354.3 57.2 %while.228 = (s32[]{:T(128)}, f32[8,1024]{1,0:T(8,128)S(1)}, f32[8,1024]{1,0:T(8,128)S(1)}, f32[8,1024]{1,0:T(8,128)S(1)}, f32[8,1024]{1,0:T(8,128)S(1)}, /*inde...) while((s32[]{:T(128)}, f32[8,1024]{1,0:T(8,128)S(1)}, ...), condition=%wide.region_3.4_spmd.clone, body=%wide.region_2.3_spmd.clone.sunk | while | flops 278532 | bytes 753807 | solution.py:39
  414.9 78.3 %all-gather.19.cloned.1.call-done = f32[64,8,1024]{2,1,0:T(8,128)} async-done(((f32[1,8,1024]{2,1,0:T(8,128)}), f32[64,8,1024]{2,1,0:T(8,128)}) %all-gather.19.cloned.1.call-update) | async-done | bytes 2097168 | tf_op jit(solution)/shard_map/all_gather | solution.py:27
  493.2 84.4 %all-gather.17.cloned.1.call-done = f32[64,8,1024]{2,1,0:T(8,128)} async-done(((f32[1,8,1024]{2,1,0:T(8,128)}), f32[64,8,1024]{2,1,0:T(8,128)}) %all-gather.17.cloned.1.call-update) | async-done | bytes 2097168 | tf_op jit(solution)/shard_map/all_gather | solution.py:27
  577.7 51.1 %while.230 = (s32[]{:T(128)}, f32[8,1024]{1,0:T(8,128)S(1)}, s32[]{:T(128)}, f32[64,8,1024]{2,1,0:T(8,128)}, f32[64,8,1024]{2,1,0:T(8,128)}, /*index=5*/s32[]{:T(128)}, s32[]{:T(128)}) while((s32[]{:T(128)}, f32[8,1024]{1,0:T(8,128)S(1)}, s32[]{:T(128)}, f32[64,8,1024]{2,1,0:T(8,128)}, f32[64,8,1024]{2,1,0:T(8,128)}, ...), condition=%wide.region_10.11_spmd.clone, body=%wide.region_9.10_spmd.clone.sunk | while | flops 32772 | bytes 131173 | solution.py:39
  629.6 32.6 %all-gather.21.cloned.1.call-done = f32[64,8,1024]{2,1,0:T(8,128)} async-done(((f32[1,8,1024]{2,1,0:T(8,128)}), f32[64,8,1024]{2,1,0:T(8,128)}) %all-gather.21.cloned.1.call-update) | async-done | bytes 2097168 | tf_op jit(solution)/shard_map/all_gather | solution.py:27
  664.0 82.8 %all-gather.23.cloned.1.call-done = f32[64,8,1024]{2,1,0:T(8,128)} async-done(((f32[1,8,1024]{2,1,0:T(8,128)}), f32[64,8,1024]{2,1,0:T(8,128)}) %all-gather.23.cloned.1.call-update) | async-done | bytes 2097168 | tf_op jit(solution)/shard_map/all_gather | solution.py:27
  750.0 48.3 %while.232 = (s32[]{:T(128)}, f32[8,1024]{1,0:T(8,128)S(1)}, s32[]{:T(128)}, f32[64,8,1024]{2,1,0:T(8,128)S(1)}, f32[64,8,1024]{2,1,0:T(8,128)}, /*index=5*/s32[]{:T(128)}, s32[]{:T(128)}) while((s32[]{:T(128)}, f32[8,1024]{1,0:T(8,128)S(1)}, s32[]{:T(128)}, f32[64,8,1024]{2,1,0:T(8,128)S(1)}, f32[64,8,1024]{2,1,0:T(8,128)}, ...), condition=%wide.region_15.16_spmd.clone, body=%wide.region_14.15_spmd.clone.sunk | while | flops 32772 | bytes 131173 | solution.py:39
  799.7 4.0 collective-permute-start.1
  811.9 100.5 %all-reduce.4 = (f32[]{:T(128)}, f32[]{:T(128)}) all-reduce(f32[]{:T(128)} %get-tuple-element.1530, f32[]{:T(128)} %get-tuple-element.1529), channel_id=1, replica_groups=mesh['tm'=64,'rows'=8] {'tm','rows'}, use_global_device_ids=true, to_apply=%region_17.18 | all-reduce | flops 2 | bytes 16 | tf_op jit(solution)/shard_map/psum | solution.py:118
  914.5 78.8 %all-gather.25.cloned.1.call-done = f32[64,8,1024]{2,1,0:T(8,128)} async-done(((f32[1,8,1024]{2,1,0:T(8,128)}), f32[64,8,1024]{2,1,0:T(8,128)}) %all-gather.25.cloned.1.call-update) | async-done | bytes 2097168 | tf_op jit(solution)/shard_map/all_gather | solution.py:27
  993.3 51.1 %while.234 = (s32[]{:T(128)}, f32[8,1024]{1,0:T(8,128)S(1)}, s32[]{:T(128)}, f32[64,8,1024]{2,1,0:T(8,128)}, f32[64,8,1024]{2,1,0:T(8,128)}, /*index=5*/s32[]{:T(128)}, s32[]{:T(128)}) while((s32[]{:T(128)}, f32[8,1024]{1,0:T(8,128)S(1)}, s32[]{:T(128)}, f32[64,8,1024]{2,1,0:T(8,128)}, f32[64,8,1024]{2,1,0:T(8,128)}, ...), condition=%wide.region_23.24_spmd.clone, body=%wide.region_22.23_spmd.clone.sunk | while | flops 32772 | bytes 131173 | solution.py:39
  1045.3 80.7 %all-gather.27.cloned.1.call-done = f32[64,8,1024]{2,1,0:T(8,128)} async-done(((f32[1,8,1024]{2,1,0:T(8,128)}), f32[64,8,1024]{2,1,0:T(8,128)}) %all-gather.27.cloned.1.call-update) | async-done | bytes 2097168 | tf_op jit(solution)/shard_map/all_gather | solution.py:27
  1129.2 48.3 %while.236 = (s32[]{:T(128)}, f32[8,1024]{1,0:T(8,128)S(1)}, s32[]{:T(128)}, f32[64,8,1024]{2,1,0:T(8,128)S(1)}, f32[64,8,1024]{2,1,0:T(8,128)}, /*index=5*/s32[]{:T(128)}, s32[]{:T(128)}) while((s32[]{:T(128)}, f32[8,1024]{1,0:T(8,128)S(1)}, s32[]{:T(128)}, f32[64,8,1024]{2,1,0:T(8,128)S(1)}, f32[64,8,1024]{2,1,0:T(8,128)}, ...), condition=%wide.region_27.28_spmd.clone, body=%wide.region_26.27_spmd.clone.sunk | while | flops 32772 | bytes 131173 | solution.py:39
  1178.2 96.2 %psum.30 = f32[]{:T(128)} all-reduce(f32[]{:T(128)} %multiply_reduce_fusion.1), channel_id=1, replica_groups=mesh['tm'=64,'rows'=8] {'tm','rows'}, use_global_device_ids=true, to_apply=%region_29.30 | all-reduce | flops 1 | bytes 8 | tf_op jit(solution)/shard_map/psum | solution.py:118
  1277.0 4.0 collective-permute-start.5
  1289.8 99.4 %psum.31 = f32[]{:T(128)} all-reduce(f32[]{:T(128)} %get-tuple-element.1727), channel_id=1, replica_groups=mesh['tm'=64,'rows'=8] {'tm','rows'}, use_global_device_ids=true, to_apply=%region_31.32 | all-reduce | flops 1 | bytes 8 | tf_op jit(solution)/shard_map/psum | solution.py:122
  1392.0 80.4 %all-gather.29.cloned.1.call-done = f32[64,8,1024]{2,1,0:T(8,128)} async-done(((f32[1,8,1024]{2,1,0:T(8,128)}), f32[64,8,1024]{2,1,0:T(8,128)}) %all-gather.29.cloned.1.call-update) | async-done | bytes 2097168 | tf_op jit(solution)/shard_map/all_gather | solution.py:27
  1472.5 51.1 %while.238 = (s32[]{:T(128)}, f32[8,1024]{1,0:T(8,128)S(1)}, s32[]{:T(128)}, f32[64,8,1024]{2,1,0:T(8,128)}, f32[64,8,1024]{2,1,0:T(8,128)}, /*index=5*/s32[]{:T(128)}, s32[]{:T(128)}) while((s32[]{:T(128)}, f32[8,1024]{1,0:T(8,128)S(1)}, s32[]{:T(128)}, f32[64,8,1024]{2,1,0:T(8,128)}, f32[64,8,1024]{2,1,0:T(8,128)}, ...), condition=%wide.region_35.36_spmd.clone, body=%wide.region_34.35_spmd.clone.sunk | while | flops 32772 | bytes 131173 | solution.py:39
  1524.3 80.8 %all-gather.31.cloned.1.call-done = f32[64,8,1024]{2,1,0:T(8,128)} async-done(((f32[1,8,1024]{2,1,0:T(8,128)}), f32[64,8,1024]{2,1,0:T(8,128)}) %all-gather.31.cloned.1.call-update) | async-done | bytes 2097168 | tf_op jit(solution)/shard_map/all_gather | solution.py:27
  1608.3 48.3 %while.240 = (s32[]{:T(128)}, f32[8,1024]{1,0:T(8,128)S(1)}, s32[]{:T(128)}, f32[64,8,1024]{2,1,0:T(8,128)S(1)}, f32[64,8,1024]{2,1,0:T(8,128)}, /*index=5*/s32[]{:T(128)}, s32[]{:T(128)}) while((s32[]{:T(128)}, f32[8,1024]{1,0:T(8,128)S(1)}, s32[]{:T(128)}, f32[64,8,1024]{2,1,0:T(8,128)S(1)}, f32[64,8,1024]{2,1,0:T(8,128)}, ...), condition=%wide.region_39.40_spmd.clone, body=%wide.region_38.39_spmd.clone.sunk | while | flops 32772 | bytes 131173 | solution.py:39
  (655 shorter events, 393.8 us)
Async XLA Ops:
  7.2 94.1 %all-gather.33.cloned.1.call-start = ((), (), s32[]{:S(2)}) async-start(), calls=%async_computation.8 | async-start | bytes 2129920 | tf_op jit(solution)/shard_map/all_gather | solution.py:27
  9.8 176.1 %all-gather.35.cloned.1.call-start = ((), (), s32[]{:S(2)}) async-start(), calls=%async_computation.9 | async-start | bytes 2129920 | tf_op jit(solution)/shard_map/all_gather | solution.py:27
  10.5 259.9 %all-gather.37.cloned.1.call-start = ((), (), s32[]{:S(2)}) async-start(), calls=%async_computation.10 | async-start | bytes 2129920 | tf_op jit(solution)/shard_map/all_gather | solution.py:27
  11.3 343.0 %all-gather.39.cloned.1.call-start = ((), (), s32[]{:S(2)}) async-start(), calls=%async_computation.11 | async-start | bytes 2129920 | tf_op jit(solution)/shard_map/all_gather | solution.py:27
  11.8 481.4 %all-gather.19.cloned.1.call-start = ((), (), s32[]{:S(2)}) async-start(), calls=%async_computation.1 | async-start | bytes 2129920 | tf_op jit(solution)/shard_map/all_gather | solution.py:27
  354.3 57.4 %copy-start.4 = (s32[2,8,1024]{2,1,0:T(8,128)S(1)}, s32[2,8,1024]{2,1,0:T(8,128)}, u32[]{:S(2)}) copy-start(s32[2,8,1024]{2,1,0:T(8,128)} %param.39) | copy-start | bytes 196612
  354.3 57.4 %copy-start.6 = (f32[2,8,1024]{2,1,0:T(8,128)S(1)}, f32[2,8,1024]{2,1,0:T(8,128)}, u32[]{:S(2)}) copy-start(f32[2,8,1024]{2,1,0:T(8,128)} %param.38) | copy-start | bytes 196612
  354.3 57.4 %copy-start.7 = (f32[2,8,1024]{2,1,0:T(8,128)S(1)}, f32[2,8,1024]{2,1,0:T(8,128)}, u32[]{:S(2)}) copy-start(f32[2,8,1024]{2,1,0:T(8,128)} %param.37) | copy-start | bytes 196612
  354.3 57.4 %copy-start.8 = (f32[2,8,1024]{2,1,0:T(8,128)S(1)}, f32[2,8,1024]{2,1,0:T(8,128)}, u32[]{:S(2)}) copy-start(f32[2,8,1024]{2,1,0:T(8,128)} %param.36) | copy-start | bytes 196612
  412.5 165.2 %all-gather.17.cloned.1.call-start = ((), (), s32[]{:S(2)}) async-start(), calls=%async_computation | async-start | bytes 2129920 | tf_op jit(solution)/shard_map/all_gather | solution.py:27
  413.6 248.6 %all-gather.21.cloned.1.call-start = ((), (), s32[]{:S(2)}) async-start(), calls=%async_computation.2 | async-start | bytes 2129920 | tf_op jit(solution)/shard_map/all_gather | solution.py:27
  414.8 332.0 %all-gather.23.cloned.1.call-start = ((), (), s32[]{:S(2)}) async-start(), calls=%async_computation.3 | async-start | bytes 2129920 | tf_op jit(solution)/shard_map/all_gather | solution.py:27
  629.5 363.8 %all-gather.25.cloned.1.call-start = ((), (), s32[]{:S(2)}) async-start(), calls=%async_computation.4 | async-start | bytes 2129920 | tf_op jit(solution)/shard_map/all_gather | solution.py:27
  798.4 5.4 collective-permute-start
  799.7 4.8 collective-permute-start.1
  804.6 5.6 collective-permute-start.2
  807.9 3.3 collective-permute-start.3
  914.5 211.5 %all-gather.27.cloned.1.call-start = ((), (), s32[]{:S(2)}) async-start(), calls=%async_computation.5 | async-start | bytes 2129920 | tf_op jit(solution)/shard_map/all_gather | solution.py:27
  1045.2 427.2 %all-gather.29.cloned.1.call-start = ((), (), s32[]{:S(2)}) async-start(), calls=%async_computation.6 | async-start | bytes 2129920 | tf_op jit(solution)/shard_map/all_gather | solution.py:27
  1275.7 5.4 collective-permute-start.4
  1277.0 4.8 collective-permute-start.5
  1281.9 6.3 collective-permute-start.6
  1285.6 3.6 collective-permute-start.7
  1392.0 213.1 %all-gather.31.cloned.1.call-start = ((), (), s32[]{:S(2)}) async-start(), calls=%async_computation.7 | async-start | bytes 2129920 | tf_op jit(solution)/shard_map/all_gather | solution.py:27
  (5 other events, 9.6 us)
Sparse Core Ops, SparseCore 0:
  11.9 89.2 all-gather.32
  105.2 80.6 all-gather.34
  189.8 80.6 all-gather.36
  273.6 80.6 all-gather.38
  412.6 80.5 all-gather.18
  497.0 80.6 all-gather.16
  581.6 80.6 all-gather.20
  666.2 80.6 all-gather.22
  914.6 78.6 all-gather.24
  1045.3 80.5 all-gather.26
  1392.1 80.3 all-gather.28
  1524.5 80.5 all-gather.30
where the time goes:
time: 1700 us; the launch traced here: 1660 us
  waiting for transfers between devices  947 us (56%)
  other arithmetic  356 us (21%)
  blocking collectives  296 us (17%)
  starting transfers between devices  22.9 us (1%)
  between operations  18.9 us (1%)
  local copies, waits for them, and re-layouts  17.1 us (1%)
    all_gather x12, waiting for transfers between devices, carried_in(): pieces = jax.tree.map(lambda part: lax.all_gather(part, axis), value)  941 us
    select_n x504, other arithmetic, turn(): jnp.where(position < mine, new, old)  349 us
    psum x2, blocking collectives, inner_total(): return lax.psum(jnp.sum(value_list), ('tm', 'rows'))  197 us
    psum x1, blocking collectives, curve_total(): return lax.psum(jnp.sum(value_list), ('tm', 'rows'))  99.4 us
  transfers between devices with their start and end apart: 20, of which 16 were waited for; matrix products, arithmetic and copies ran while one was open for 3% of the time, Pallas kernels for 0%

commit v1 on v0

v1 whole, which is shorter than its diff:
```python
import jax
import jax.numpy as jnp
from jax import lax
from jax.experimental import pallas as pl
from jax.experimental.pallas import tpu as pltpu
from jax.sharding import PartitionSpec as P

RHO = 0.995
RHO_SQ = RHO * RHO
MESH = pl.DeviceIdType.MESH
F32 = jnp.float32
NT = 64
NY = 8
LEVELS = 7


def patch_of(m):
    x, z, c = m // 16, (m // 2) % 8, m % 2
    odd = x % 2
    return 16 * x + 2 * (z + odd * (7 - 2 * z)) + c


def device_of(j):
    return patch_of(j)


def iota(shape, axis):
    return lax.broadcasted_iota(jnp.int32, shape, axis)


def swap_blocks(v):
    shape, sub, lane = v.shape, v.ndim - 2, v.ndim - 1
    s, g = iota(shape, sub), iota(shape, lane) // 16
    for b in (1, 2, 4):
        down = pltpu.roll(pltpu.roll(v, 8 - b, sub), 16 * b, lane)
        s_b, g_b = (s // b) % 2, (g // b) % 2
        if b == 4:
            v = jnp.where(s_b == g_b, v, down)
        else:
            up = pltpu.roll(pltpu.roll(v, b, sub), 128 - 16 * b, lane)
            v = jnp.where(s_b == g_b, v, jnp.where(s_b == 0, down, up))
    return v


def lane_sum(v):
    return jnp.sum(v, axis=1, keepdims=True)


def fold(v):
    return jnp.sum(v.reshape(v.shape[0] // 8, 8, 128), axis=0)


def kernel(
    obs_ref, noise_ref, prior_ref, mask_ref, kappa_ref, prec_ref,
    x_ref, r_ref, p_ref,
    s_mask, s_right, b_mask, b_right, stencil, omega, gain, last, rc, nc,
    s_z, s_one, s_two, b_z, b_one, b_two, pads, cols_out, side_in, rows_in,
    sums_y, sums_t, mine, one_row,
    send_big, recv_big, halo_send, halo_recv, sum_send, sum_recv, own_sem,
):
    me, y = lax.axis_index("tm"), lax.axis_index("rows")
    j = patch_of(me)

    barrier = pltpu.get_barrier_semaphore()

    def greet(k, carry):
        t = lax.rem(me + k, NT)
        pl.semaphore_signal(barrier, inc=1, device_id={"tm": t}, device_id_type=MESH)
        return carry

    lax.fori_loop(1, NT, greet, 0)

    def greet_rows(k, carry):
        t = lax.rem(y + k, NY)
        pl.semaphore_signal(barrier, inc=1, device_id={"rows": t}, device_id_type=MESH)
        return carry

    lax.fori_loop(1, NY, greet_rows, 0)

    for tile in range(8):
        cols = slice(128 * tile, 128 * tile + 128)
        mask = mask_ref[:, :, cols].astype(F32)
        prec = prec_ref[:, cols][None]
        right = mask * (prec * obs_ref[:, :, cols] + jnp.sqrt(prec) * noise_ref[:, :, cols])
        right = right + prior_ref[:, :, cols]
        r_ref[:, :, cols] = right
        mask, right = swap_blocks(mask), swap_blocks(right)
        for h in range(2):
            s_mask[pl.ds(16 * tile + h, 8, stride=2), :] = mask[h]
            s_right[pl.ds(16 * tile + h, 8, stride=2), :] = right[h]

    pl.semaphore_wait(barrier, NT - 1 + NY - 1)

    def to_patches(src, dst, slot):
        def send(i, carry):
            t = lax.rem(me + 1 + lax.rem(i + 23, NT - 1), NT)
            pltpu.make_async_remote_copy(
                src_ref=src.at[pl.ds(2 * patch_of(t), 2)],
                dst_ref=dst.at[pl.ds(2 * me, 2)],
                send_sem=send_big.at[slot],
                recv_sem=recv_big.at[slot],
                device_id={"tm": t},
                device_id_type=MESH,
            ).start()
            return carry

        lax.fori_loop(0, NT - 1, send, 0)
        own = pltpu.make_async_copy(
            src.at[pl.ds(2 * j, 2)], dst.at[pl.ds(2 * me, 2)], own_sem.at[slot]
        )
        own.start()
        return own

    def to_hours(src, dst, slot, rows):
        def send(i, carry):
            t = lax.rem(me + 1 + lax.rem(i + 23, NT - 1), NT)
            pltpu.make_async_remote_copy(
                src_ref=src.at[pl.ds(rows * t, rows)],
                dst_ref=dst.at[pl.ds(rows * j, rows)],
                send_sem=send_big.at[slot],
                recv_sem=recv_big.at[slot],
                device_id={"tm": t},
                device_id_type=MESH,
            ).start()
            return carry

        lax.fori_loop(0, NT - 1, send, 0)
        own = pltpu.make_async_copy(
            src.at[pl.ds(rows * me, rows)], dst.at[pl.ds(rows * j, rows)], own_sem.at[slot]
        )
        own.start()
        return own

    def big(src, dst, slot, rows):
        n = rows * (NT - 1)
        return pltpu.make_async_remote_copy(
            src_ref=src.at[pl.ds(0, n)],
            dst_ref=dst.at[pl.ds(0, n)],
            send_sem=send_big.at[slot],
            recv_sem=recv_big.at[slot],
            device_id={"tm": lax.rem(me + 1, NT)},
            device_id_type=MESH,
        )

    own_mask = to_patches(s_mask, b_mask, 0)
    own_right = to_patches(s_right, b_right, 1)

    tile, back = j // 8, j % 8
    shift = lax.rem(128 - 16 * back, 128)
    columns = pl.ds(pl.multiple_of(tile * 128, 128), 128)

    def per_cell(ref):
        rows = pltpu.roll(ref[:, columns], shift, 1)
        turned = jnp.concatenate([rows, jnp.zeros((120, 128), F32)], axis=0).T
        return [jnp.broadcast_to(turned[0:16, r : r + 1], (16, 128)) for r in range(8)]

    kappa, prec = per_cell(kappa_ref), per_cell(prec_ref)
    for r in range(8):
        diag = 1.0 / (kappa[r] + 4.0)
        stencil[pl.ds(16 * r, 16), :] = diag
        omega[pl.ds(16 * r, 16), :] = prec[r] * diag

    own_mask.wait()
    big(s_mask, b_mask, 0, 2).wait_recv()
    omega[...] = omega[...] * b_mask[...].T

    def factor(i, carry):
        at = pl.ds(pl.multiple_of(32 * i, 32), 32)
        lane = iota((32, 128), 1)
        w = omega[at, :]
        first = lane == 0
        a = jnp.where(first, 0.0, w + RHO_SQ)
        b = w
        c = jnp.where(first, 0.0, 1.0)
        d = jnp.ones_like(w)
        for k in range(LEVELS):
            s = 1 << k
            keep = lane < s
            pb, pd = pltpu.roll(b, s, 1), pltpu.roll(d, s, 1)
            nb, nd = a * pb + b * pd, c * pb + d * pd
            if k < LEVELS - 1:
                pa, pc = pltpu.roll(a, s, 1), pltpu.roll(c, s, 1)
                na, nc_ = a * pa + b * pc, c * pa + d * pc
                a, c = jnp.where(keep, a, na), jnp.where(keep, c, nc_)
            b, d = jnp.where(keep, b, nb), jnp.where(keep, d, nd)
            if k == LEVELS - 2:
                scale = 1.0 / (c + d)
                a, b, c, d = a * scale, b * scale, c * scale, d * scale
        sigma = b / d
        before = pltpu.roll(sigma, 1, 1)
        final = lane == 127
        pivot = jnp.where(final, w + ((1.0 - RHO_SQ) + before) / (1.0 + before), 1.0 + sigma)
        inverse = 1.0 / pivot
        last[at, :] = inverse
        g = pltpu.roll(jnp.where(final, 0.0, RHO * inverse), 1, 1)
        for k in range(LEVELS):
            gain[k, at, :] = g
            if k < LEVELS - 1:
                g = g * pltpu.roll(g, 1 << k, 1)
        return carry

    lax.fori_loop(0, 4, factor, 0)

    def solve(v):
        v = v * stencil[...]
        for k in range(LEVELS):
            v = v + gain[k] * pltpu.roll(v, 1 << k, 1)
        v = v * last[...]
        for k in range(LEVELS):
            v = v + pltpu.roll(gain[k] * v, 128 - (1 << k), 1)
        return v

    left, right_dev = device_of(lax.rem(j + NT - 1, NT)), device_of(lax.rem(j + 1, NT))
    above, below = lax.rem(y + NY - 1, NY), lax.rem(y + 1, NY)

    def halo_copies(n):
        pad = pads.at[n]
        parts = (
            (pad.at[pl.ds(8, 16)], rows_in.at[n, 1], {"rows": above}),
            (pad.at[pl.ds(32 * 7 + 8, 16)], rows_in.at[n, 0], {"rows": below}),
            (cols_out.at[n, 0], side_in.at[n, 1], {"tm": left}),
            (cols_out.at[n, 1], side_in.at[n, 0], {"tm": right_dev}),
        )
        return [
            pltpu.make_async_remote_copy(
                src_ref=src,
                dst_ref=dst,
                send_sem=halo_send.at[4 * n + i],
                recv_sem=halo_recv.at[4 * n + i],
                device_id=to,
                device_id_type=MESH,
            )
            for i, (src, dst, to) in enumerate(parts)
        ]

    def halo_start(n, v):
        for r in range(8):
            pads[n, pl.ds(32 * r + 8, 16), :] = v[16 * r : 16 * r + 16]
        cols_out[n, 0] = pads[n, pl.ds(8, 8, stride=32), :]
        cols_out[n, 1] = pads[n, pl.ds(23, 8, stride=32), :]
        copies = halo_copies(n)
        for copy in copies:
            copy.start()
        return copies

    hour = iota((16, 128), 1)
    from_before = jnp.where(hour == 0, 0.0, RHO).astype(F32)
    from_after = jnp.where(hour == 127, 0.0, RHO).astype(F32)
    weight = jnp.where((hour == 0) | (hour == 127), 1.0, 1.0 + RHO_SQ).astype(F32)

    def neighbours(n, copies):
        for copy in copies:
            copy.wait_recv()
        pads[n, pl.ds(7, 8, stride=32), :] = jnp.where(j == 0, 0.0, side_in[n, 0])
        pads[n, pl.ds(24, 8, stride=32), :] = jnp.where(j == NT - 1, 0.0, side_in[n, 1])
        for r in range(8):
            if r == 0:
                up = jnp.where(y == 0, 0.0, rows_in[n, 0])
            else:
                up = pads[n, pl.ds(32 * (r - 1) + 8, 16), :]
            if r == 7:
                down = jnp.where(y == NY - 1, 0.0, rows_in[n, 1])
            else:
                down = pads[n, pl.ds(32 * (r + 1) + 8, 16), :]
            u = pads[n, pl.ds(32 * r + 7, 16), :] + pads[n, pl.ds(32 * r + 9, 16), :]
            u = u + (up + down)
            u = weight * u - (
                from_before * pltpu.roll(u, 1, 1) + from_after * pltpu.roll(u, 127, 1)
            )
            nc[pl.ds(16 * r, 16), :] = u
        return nc[...]

    own_right.wait()
    big(s_right, b_right, 1, 2).wait_recv()
    rc[...] = b_right[...].T
    z0 = solve(rc[...])
    copies_0 = halo_start(0, z0)
    s_z[...] = z0.T
    own_z = to_hours(s_z, b_z, 2, 2)
    rz_part = fold(rc[...] * z0)

    n0 = neighbours(0, copies_0)
    s0 = solve(n0)
    copies_1 = halo_start(1, s0)

    def interleave(ref, even, odd):
        ref[pl.ds(0, 128, stride=2), :] = even.T
        ref[pl.ds(1, 128, stride=2), :] = odd.T

    interleave(s_one, n0, s0)
    own_one = to_hours(s_one, b_one, 3, 4)
    e1_part = fold(rc[...] * s0)
    e2_part = fold(n0 * s0)

    n1 = neighbours(1, copies_1)
    e3_part = fold(n1 * jnp.concatenate([pads[1, pl.ds(32 * r + 8, 16), :] for r in range(8)], axis=0))

    sub = iota((8, 128), 0)
    total = jnp.zeros((8, 128), F32)
    for i, part in enumerate((rz_part, e1_part, e2_part, e3_part)):
        total = jnp.where(sub == i, jnp.sum(part, axis=0, keepdims=True), total)
    mine[...] = total
    sums_y[pl.ds(pl.multiple_of(8 * y, 8), 8), :] = total

    def rows_copy(t):
        return pltpu.make_async_remote_copy(
            src_ref=mine,
            dst_ref=sums_y.at[pl.ds(pl.multiple_of(8 * y, 8), 8)],
            send_sem=sum_send.at[0],
            recv_sem=sum_recv.at[0],
            device_id={"rows": t},
            device_id_type=MESH,
        )

    def send_rows(k, carry):
        rows_copy(lax.rem(y + k, NY)).start()
        return carry

    lax.fori_loop(1, NY, send_rows, 0)

    s1 = solve(n1)
    interleave(s_two, n1, s1)
    own_two = to_hours(s_two, b_two, 4, 4)

    def all_rows(n, src, dst, slot):
        return pltpu.make_async_remote_copy(
            src_ref=src.at[pl.ds(0, n)],
            dst_ref=dst.at[pl.ds(0, n)],
            send_sem=sum_send.at[slot],
            recv_sem=sum_recv.at[slot],
            device_id={"rows": lax.rem(y + 1, NY)},
            device_id_type=MESH,
        )

    all_rows(8 * (NY - 1), sums_y, sums_y, 0).wait_recv()
    part = fold(sums_y[...])
    part = part + pltpu.roll(part, 64, 1)
    part = part + pltpu.roll(part, 32, 1)
    part = jnp.where(iota((8, 128), 1) // 32 == sub, part, 0.0)
    one_row[...] = jnp.broadcast_to(jnp.sum(part, axis=0, keepdims=True), (8, 128))
    sums_t[pl.ds(me, 1), :] = one_row[0:1, :]

    def send_sums(i, carry):
        t = lax.rem(me + 1 + lax.rem(i + 23, NT - 1), NT)
        pltpu.make_async_remote_copy(
            src_ref=one_row.at[pl.ds(0, 1)],
            dst_ref=sums_t.at[pl.ds(me, 1)],
            send_sem=sum_send.at[1],
            recv_sem=sum_recv.at[1],
            device_id={"tm": t},
            device_id_type=MESH,
        ).start()
        return carry

    lax.fori_loop(0, NT - 1, send_sums, 0)

    own_z.wait()
    big(s_z, b_z, 2, 2).wait_recv()
    own_one.wait()
    big(s_one, b_one, 3, 4).wait_recv()
    own_two.wait()
    big(s_two, b_two, 4, 4).wait_recv()
    for ref, stride in ((b_z, 2), (b_one, 4), (b_two, 4)):
        for tile in range(8):
            for o in range(stride):
                at = pl.ds(8 * stride * tile + o, 8, stride=stride)
                ref[at, :] = swap_blocks(ref[at, :])

    all_rows(NT - 1, sums_t, sums_t, 1).wait_recv()
    sums = jnp.sum(fold(sums_t[...]), axis=0, keepdims=True)
    group = iota((1, 128), 1) // 32
    rz0, e1, e2, e3 = [lane_sum(jnp.where(group == i, sums, 0.0)) for i in range(4)]
    curved = rz0 - e1
    alpha0 = rz0 / curved
    beta0 = (e2 * rz0 - e1 * e1) / (curved * curved)
    along = 1.0 + beta0 - alpha0
    curved1 = along * along * curved + 2.0 * along * alpha0 * (e1 - e2) + alpha0 * alpha0 * (e2 - e3)
    alpha1 = beta0 * rz0 / curved1
    first = alpha0 + alpha1 * (1.0 + beta0)
    second = alpha0 * alpha1
    c0, c1 = 1.0 - first + second, first - 2.0 * second

    for tile in range(8):
        cols = slice(128 * tile, 128 * tile + 128)
        for h in range(2):
            z = b_z[pl.ds(16 * tile + h, 8, stride=2), :]
            n_a = b_one[pl.ds(32 * tile + 2 * h, 8, stride=4), :]
            s_a = b_one[pl.ds(32 * tile + 2 * h + 1, 8, stride=4), :]
            n_b = b_two[pl.ds(32 * tile + 2 * h, 8, stride=4), :]
            s_b = b_two[pl.ds(32 * tile + 2 * h + 1, 8, stride=4), :]
            x_ref[h, :, cols] = (first - second) * z + second * s_a
            r_ref[h, :, cols] = c0 * r_ref[h, :, cols] + c1 * n_a + second * n_b
            p_ref[h, :, cols] = c0 * z + c1 * s_a + second * s_b

    for copy in copies_0 + copies_1:
        copy.wait_send()
    big(s_mask, b_mask, 0, 2).wait_send()
    big(s_right, b_right, 1, 2).wait_send()
    big(s_z, b_z, 2, 2).wait_send()
    big(s_one, b_one, 3, 4).wait_send()
    big(s_two, b_two, 4, 4).wait_send()
    all_rows(8 * (NY - 1), sums_y, sums_y, 0).wait_send()
    all_rows(NT - 1, sums_t, sums_t, 1).wait_send()


def per_device(observations, obs_noise, prior_noise, observed, kappa_sq, obs_precision):
    vmem = pl.BlockSpec(memory_space=pltpu.VMEM)
    out = jax.ShapeDtypeStruct(observations.shape, F32)

    def buf(*shape):
        return pltpu.VMEM(shape, F32)

    return pl.pallas_call(
        kernel,
        out_shape=(out, out, out),
        in_specs=[vmem] * 6,
        out_specs=(vmem,) * 3,
        scratch_shapes=[
            buf(128, 128), buf(128, 128), buf(128, 128), buf(128, 128),
            buf(128, 128), buf(128, 128), buf(LEVELS, 128, 128), buf(128, 128),
            buf(128, 128), buf(128, 128),
            buf(128, 128), buf(256, 128), buf(256, 128),
            buf(128, 128), buf(256, 128), buf(256, 128),
            buf(2, 256, 128), buf(2, 2, 8, 128), buf(2, 2, 8, 128), buf(2, 2, 16, 128),
            buf(64, 128), buf(64, 128), buf(8, 128), buf(8, 128),
            pltpu.SemaphoreType.DMA((5,)), pltpu.SemaphoreType.DMA((5,)),
            pltpu.SemaphoreType.DMA((8,)), pltpu.SemaphoreType.DMA((8,)),
            pltpu.SemaphoreType.DMA((2,)), pltpu.SemaphoreType.DMA((2,)),
            pltpu.SemaphoreType.DMA((5,)),
        ],
        compiler_params=pltpu.CompilerParams(collective_id=0, has_side_effects=True),
    )(observations, obs_noise, prior_noise, observed, kappa_sq, obs_precision)


def solution(mesh):
    in_specs = (P("tm", "rows", None),) * 4 + (P("rows", None),) * 2
    out_specs = (P("tm", "rows", None),) * 3
    return jax.shard_map(
        per_device, mesh=mesh, in_specs=in_specs, out_specs=out_specs, check_vma=False
    )
```

time: 1700 us -> 55.5 us (0.03); the launches traced: 1660 us -> 55.3 us
  waiting for transfers between devices: 947 us -> 0 us
  other arithmetic: 356 us -> 0 us
  blocking collectives: 296 us -> 0 us
  Pallas kernels: 0 us -> 51.6 us
  starting transfers between devices: 22.9 us -> 0 us
  between operations: 18.9 us -> 0.65 us
    all_gather x12 -> x0, waiting for transfers between devices: 941 us -> none  [carried_in(): pieces = jax.tree.map(lambda part: lax.all_gather(part, axis), value)]
    select_n x505 -> x0, other arithmetic: 349 us -> none  [the longest x504 349 us: turn(): jnp.where(position < mine, new, old)]
    psum x3 -> x0, blocking collectives: 296 us -> none  [the longest x2 197 us: inner_total(): return lax.psum(jnp.sum(value_list), ('tm', 'rows'))]
    pallas_call x0 -> x1, Pallas kernels: none -> 51.6 us  [per_device(): pl.pallas_call(kernel, out_shape=(out, out, out), in_specs=[vmem] * 6, ou...]
    ppermute x8 -> x0, starting transfers between devices: 22.4 us -> none  [the longest x4 12.8 us: with_halo(): before = lax.ppermute(last, axis, up)]
  transfers between devices with their start and end apart: 20 -> 0, of which waited for: 16 -> 0; matrix products, arithmetic and copies ran while one was open for 3% -> 0% of each run, Pallas kernels for 0% -> 0%
where the time goes in v1:
time: 55.5 us; the launch traced here: 55.3 us
  Pallas kernels  51.6 us (93%)
  local copies, waits for them, and re-layouts  3 us (5%)
  between operations  0.65 us (1%)
    pallas_call x1, Pallas kernels, per_device(): pl.pallas_call(kernel, out_shape=(out, out, out), in_specs=[vmem] * 6, ou...  51.6 us
    unnamed x7, local copies, waits for them, and re-layouts  3 us

profile of v1, /device:TPU:1, one launch (start us, length us, event | category | flops | bytes accessed | tf_op | source)
XLA Modules:
  0.0 55.3 jit_solution(16567575499113391148)
XLA Ops:
  0.6 51.6 %shard_map.85 = (f32[2,8,1024]{2,1,0:T(8,128)}, f32[2,8,1024]{2,1,0:T(8,128)}, f32[2,8,1024]{2,1,0:T(8,128)}) custom-call(f32[2,8,1024]{2,1,0:T(8,128)} %obs_ref.1, f32[2,8,1024]{2,1,0:T(8,128)} %noise_ref.1, f32[2,8,1024]{2,1,0:T(8,128)} %prior_ref.1, s32[2,8,1024]{2,1,0:T(8,128)} %mask_ref.1, f32[8,1024]{1,0:T(8,128)} %kappa_ref.1, f32[8,1024]{1,0:T(8,128)} %prec_ref.1), custom_call_target="tpu_custom_call" | custom-call | tf_op jit(solution)/shard_map/pallas_call | solution.py:413
  52.3 0.0 copy-start.1
  52.3 1.5 %copy.12 = f32[2,8,1024]{2,1,0:T(8,128)} copy(f32[2,8,1024]{2,1,0:T(8,128)} %get-tuple-element.6) | data formatting | bytes 131072
  53.8 0.0 copy-done.1
  53.8 0.0 copy-start
  53.8 0.6 %copy.13 = f32[2,8,1024]{2,1,0:T(8,128)} copy(f32[2,8,1024]{2,1,0:T(8,128)S(1)} %copy-done.1) | data formatting | bytes 131072
  54.4 0.2 copy-done
  54.6 0.6 %copy.14 = f32[2,8,1024]{2,1,0:T(8,128)} copy(f32[2,8,1024]{2,1,0:T(8,128)S(1)} %copy-done) | data formatting | bytes 131072
Async XLA Ops:
  52.3 1.5 %copy-start.1 = (f32[2,8,1024]{2,1,0:T(8,128)S(1)}, f32[2,8,1024]{2,1,0:T(8,128)}, u32[]{:S(2)}) copy-start(f32[2,8,1024]{2,1,0:T(8,128)} %get-tuple-element.7) | copy-start | bytes 196612
  53.8 0.9 %copy-start = (f32[2,8,1024]{2,1,0:T(8,128)S(1)}, f32[2,8,1024]{2,1,0:T(8,128)}, u32[]{:S(2)}) copy-start(f32[2,8,1024]{2,1,0:T(8,128)} %get-tuple-element.8) | copy-start | bytes 196612

commit v2 on v1

--- a/solution.py
+++ b/solution.py
@@ -22,6 +22,19 @@
 
 def device_of(j):
     return patch_of(j)
+
+
+def ring_tile(tile):
+    return tile + (0, 0, 1, -1)[tile % 4]
+
+
+def ring_order(v, tile):
+    if tile % 4 < 2:
+        return v
+    axis = v.ndim - 2
+    v = pltpu.roll(v, 4, axis)
+    even = (iota(v.shape, axis) // 2) % 2 == 0
+    return jnp.where(even, pltpu.roll(v, 6, axis), pltpu.roll(v, 2, axis))
 
 
 def iota(shape, axis):
@@ -51,31 +64,57 @@
 
 
 def kernel(
+    obs_hbm, noise_hbm, prior_hbm, mask_hbm, kappa_hbm, prec_hbm,
+    z_hbm, na_hbm, sa_hbm, nb_hbm, sb_hbm, r_hbm, coef_ref,
     obs_ref, noise_ref, prior_ref, mask_ref, kappa_ref, prec_ref,
-    x_ref, r_ref, p_ref,
-    s_mask, s_right, b_mask, b_right, stencil, omega, gain, last, rc, nc,
+    z_all, na_all, sa_all, nb_all, sb_all, r_all,
+    s_mask, s_right, b_mask, b_right, stencil, gain, last, rc, nc,
     s_z, s_one, s_two, b_z, b_one, b_two, pads, cols_out, side_in, rows_in,
     sums_y, sums_t, mine, one_row,
-    send_big, recv_big, halo_send, halo_recv, sum_send, sum_recv, own_sem,
+    send_big, recv_big, halo_send, halo_recv, sum_send, sum_recv, own_sem, in_sem, out_sem,
 ):
     me, y = lax.axis_index("tm"), lax.axis_index("rows")
     j = patch_of(me)
 
     barrier = pltpu.get_barrier_semaphore()
 
-    def greet(k, carry):
-        t = lax.rem(me + k, NT)
+    def each_peer(act):
+        def block(b, carry):
+            base = me + 22 + 7 * b + jnp.where(b >= 6, 1, 0)
+            base = base - jnp.where(base >= NT, NT, 0)
+            base = base - jnp.where(base >= NT, NT, 0)
+            for i in range(7):
+                t = base + i
+                act(t - jnp.where(t >= NT, NT, 0))
+            return carry
+
+        lax.fori_loop(0, 9, block, 0)
+
+    def greet(t):
         pl.semaphore_signal(barrier, inc=1, device_id={"tm": t}, device_id_type=MESH)
-        return carry
-
-    lax.fori_loop(1, NT, greet, 0)
-
-    def greet_rows(k, carry):
+
+    each_peer(greet)
+    for k in range(1, NY):
         t = lax.rem(y + k, NY)
         pl.semaphore_signal(barrier, inc=1, device_id={"rows": t}, device_id_type=MESH)
-        return carry
-
-    lax.fori_loop(1, NY, greet_rows, 0)
+
+    loads = [
+        pltpu.make_async_copy(src, dst, in_sem.at[i])
+        for i, (src, dst) in enumerate(
+            (
+                (mask_hbm, mask_ref),
+                (obs_hbm, obs_ref),
+                (noise_hbm, noise_ref),
+                (prior_hbm, prior_ref),
+                (prec_hbm, prec_ref),
+                (kappa_hbm, kappa_ref),
+            )
+        )
+    ]
+    for load in loads:
+        load.start()
+    for load in loads:
+        load.wait()
 
     for tile in range(8):
         cols = slice(128 * tile, 128 * tile + 128)
@@ -83,50 +122,29 @@
         prec = prec_ref[:, cols][None]
         right = mask * (prec * obs_ref[:, :, cols] + jnp.sqrt(prec) * noise_ref[:, :, cols])
         right = right + prior_ref[:, :, cols]
-        r_ref[:, :, cols] = right
-        mask, right = swap_blocks(mask), swap_blocks(right)
+        r_all[:, :, cols] = right
+        mask, right = ring_order(swap_blocks(mask), tile), ring_order(swap_blocks(right), tile)
         for h in range(2):
-            s_mask[pl.ds(16 * tile + h, 8, stride=2), :] = mask[h]
-            s_right[pl.ds(16 * tile + h, 8, stride=2), :] = right[h]
+            at = pl.ds(16 * ring_tile(tile) + h, 8, stride=2)
+            s_mask[at, :] = mask[h]
+            s_right[at, :] = right[h]
 
     pl.semaphore_wait(barrier, NT - 1 + NY - 1)
 
-    def to_patches(src, dst, slot):
-        def send(i, carry):
-            t = lax.rem(me + 1 + lax.rem(i + 23, NT - 1), NT)
+    def to_all(src, dst, slot, rows):
+        def send(t):
             pltpu.make_async_remote_copy(
-                src_ref=src.at[pl.ds(2 * patch_of(t), 2)],
-                dst_ref=dst.at[pl.ds(2 * me, 2)],
+                src_ref=src.at[pl.ds(rows * t, rows)],
+                dst_ref=dst.at[pl.ds(rows * me, rows)],
                 send_sem=send_big.at[slot],
                 recv_sem=recv_big.at[slot],
                 device_id={"tm": t},
                 device_id_type=MESH,
             ).start()
-            return carry
-
-        lax.fori_loop(0, NT - 1, send, 0)
+
+        each_peer(send)
         own = pltpu.make_async_copy(
-            src.at[pl.ds(2 * j, 2)], dst.at[pl.ds(2 * me, 2)], own_sem.at[slot]
-        )
-        own.start()
-        return own
-
-    def to_hours(src, dst, slot, rows):
-        def send(i, carry):
-            t = lax.rem(me + 1 + lax.rem(i + 23, NT - 1), NT)
-            pltpu.make_async_remote_copy(
-                src_ref=src.at[pl.ds(rows * t, rows)],
-                dst_ref=dst.at[pl.ds(rows * j, rows)],
-                send_sem=send_big.at[slot],
-                recv_sem=recv_big.at[slot],
-                device_id={"tm": t},
-                device_id_type=MESH,
-            ).start()
-            return carry
-
-        lax.fori_loop(0, NT - 1, send, 0)
-        own = pltpu.make_async_copy(
-            src.at[pl.ds(rows * me, rows)], dst.at[pl.ds(rows * j, rows)], own_sem.at[slot]
+            src.at[pl.ds(rows * me, rows)], dst.at[pl.ds(rows * me, rows)], own_sem.at[slot]
         )
         own.start()
         return own
@@ -142,8 +160,8 @@
             device_id_type=MESH,
         )
 
-    own_mask = to_patches(s_mask, b_mask, 0)
-    own_right = to_patches(s_right, b_right, 1)
+    own_mask = to_all(s_mask, b_mask, 0, 2)
+    own_right = to_all(s_right, b_right, 1, 2)
 
     tile, back = j // 8, j % 8
     shift = lax.rem(128 - 16 * back, 128)
@@ -154,52 +172,53 @@
         turned = jnp.concatenate([rows, jnp.zeros((120, 128), F32)], axis=0).T
         return [jnp.broadcast_to(turned[0:16, r : r + 1], (16, 128)) for r in range(8)]
 
-    kappa, prec = per_cell(kappa_ref), per_cell(prec_ref)
+    kappa = per_cell(kappa_ref)
     for r in range(8):
-        diag = 1.0 / (kappa[r] + 4.0)
-        stencil[pl.ds(16 * r, 16), :] = diag
-        omega[pl.ds(16 * r, 16), :] = prec[r] * diag
+        stencil[pl.ds(16 * r, 16), :] = 1.0 / (kappa[r] + 4.0)
+    one_row[...] = swap_blocks(prec_ref[:, columns] / (kappa_ref[:, columns] + 4.0))
+    ratio = one_row[pl.ds(back, 1), :]
 
     own_mask.wait()
     big(s_mask, b_mask, 0, 2).wait_recv()
-    omega[...] = omega[...] * b_mask[...].T
-
-    def factor(i, carry):
-        at = pl.ds(pl.multiple_of(32 * i, 32), 32)
-        lane = iota((32, 128), 1)
-        w = omega[at, :]
-        first = lane == 0
-        a = jnp.where(first, 0.0, w + RHO_SQ)
-        b = w
-        c = jnp.where(first, 0.0, 1.0)
-        d = jnp.ones_like(w)
-        for k in range(LEVELS):
-            s = 1 << k
-            keep = lane < s
-            pb, pd = pltpu.roll(b, s, 1), pltpu.roll(d, s, 1)
-            nb, nd = a * pb + b * pd, c * pb + d * pd
-            if k < LEVELS - 1:
-                pa, pc = pltpu.roll(a, s, 1), pltpu.roll(c, s, 1)
-                na, nc_ = a * pa + b * pc, c * pa + d * pc
-                a, c = jnp.where(keep, a, na), jnp.where(keep, c, nc_)
-            b, d = jnp.where(keep, b, nb), jnp.where(keep, d, nd)
-            if k == LEVELS - 2:
-                scale = 1.0 / (c + d)
-                a, b, c, d = a * scale, b * scale, c * scale, d * scale
-        sigma = b / d
-        before = pltpu.roll(sigma, 1, 1)
-        final = lane == 127
-        pivot = jnp.where(final, w + ((1.0 - RHO_SQ) + before) / (1.0 + before), 1.0 + sigma)
-        inverse = 1.0 / pivot
-        last[at, :] = inverse
-        g = pltpu.roll(jnp.where(final, 0.0, RHO * inverse), 1, 1)
-        for k in range(LEVELS):
-            gain[k, at, :] = g
-            if k < LEVELS - 1:
-                g = g * pltpu.roll(g, 1 << k, 1)
-        return carry
-
-    lax.fori_loop(0, 4, factor, 0)
+
+    seg = iota((8, 128), 0)
+    ones, zeros = jnp.ones((8, 128), F32), jnp.zeros((8, 128), F32)
+    w = [b_mask[pl.ds(k, 8, stride=16), :] * ratio for k in range(16)]
+    a, b, c, d = ones, zeros, zeros, ones
+    for k in range(16):
+        ac, bd = a + c, b + d
+        a, b, c, d = w[k] * ac + RHO_SQ * a, w[k] * bd + RHO_SQ * b, ac, bd
+    scale = 1.0 / (c + d)
+    a, b, c, d = a * scale, b * scale, c * scale, d * scale
+    for n in (1, 2, 4):
+        pa, pb, pc, pd = [pltpu.roll(q, n, 0) for q in (a, b, c, d)]
+        keep = seg < n
+        a, b, c, d = [
+            jnp.where(keep, old, new)
+            for old, new in zip(
+                (a, b, c, d),
+                (a * pa + b * pc, a * pb + b * pd, c * pa + d * pc, c * pb + d * pd),
+            )
+        ]
+    b = jnp.where(seg == 0, 0.0, pltpu.roll(b, 1, 0))
+    d = jnp.where(seg == 0, 1.0, pltpu.roll(d, 1, 0))
+    for k in range(16):
+        before_b, before_d = b, d
+        bd = b + d
+        b, d = w[k] * bd + RHO_SQ * b, bd
+        pivot = (b + d) / d
+        if k == 15:
+            before = before_b / before_d
+            final = w[k] + ((1.0 - RHO_SQ) + before) / (1.0 + before)
+            pivot = jnp.where(seg == 7, final, pivot)
+        rc[pl.ds(k, 8, stride=16), :] = 1.0 / pivot
+    inverse = rc[...].T
+    last[...] = inverse
+    g = pltpu.roll(jnp.where(iota((128, 128), 1) == 127, 0.0, RHO * inverse), 1, 1)
+    for k in range(LEVELS):
+        gain[k] = g
+        if k < LEVELS - 1:
+            g = g * pltpu.roll(g, 1 << k, 1)
 
     def solve(v):
         v = v * stencil[...]
@@ -276,7 +295,7 @@
     z0 = solve(rc[...])
     copies_0 = halo_start(0, z0)
     s_z[...] = z0.T
-    own_z = to_hours(s_z, b_z, 2, 2)
+    own_z = to_all(s_z, b_z, 2, 2)
     rz_part = fold(rc[...] * z0)
 
     n0 = neighbours(0, copies_0)
@@ -288,7 +307,7 @@
         ref[pl.ds(1, 128, stride=2), :] = odd.T
 
     interleave(s_one, n0, s0)
-    own_one = to_hours(s_one, b_one, 3, 4)
+    own_one = to_all(s_one, b_one, 3, 4)
     e1_part = fold(rc[...] * s0)
     e2_part = fold(n0 * s0)
 
@@ -320,7 +339,7 @@
 
     s1 = solve(n1)
     interleave(s_two, n1, s1)
-    own_two = to_hours(s_two, b_two, 4, 4)
+    own_two = to_all(s_two, b_two, 4, 4)
 
     def all_rows(n, src, dst, slot):
         return pltpu.make_async_remote_copy(
@@ -354,17 +373,34 @@
 
     lax.fori_loop(0, NT - 1, send_sums, 0)
 
-    own_z.wait()
-    big(s_z, b_z, 2, 2).wait_recv()
-    own_one.wait()
-    big(s_one, b_one, 3, 4).wait_recv()
-    own_two.wait()
-    big(s_two, b_two, 4, 4).wait_recv()
-    for ref, stride in ((b_z, 2), (b_one, 4), (b_two, 4)):
+    stores = []
+    store = pltpu.make_async_copy(r_all, r_hbm, out_sem.at[5])
+    store.start()
+    stores.append(store)
+    outs = (
+        (0, b_z, 2, 0, z_all, z_hbm),
+        (1, b_one, 4, 0, na_all, na_hbm),
+        (2, b_one, 4, 1, sa_all, sa_hbm),
+        (3, b_two, 4, 0, nb_all, nb_hbm),
+        (4, b_two, 4, 1, sb_all, sb_hbm),
+    )
+    for i, ref, stride, o, dst, hbm in outs:
+        if i == 0:
+            own_z.wait()
+            big(s_z, b_z, 2, 2).wait_recv()
+        elif i == 1:
+            own_one.wait()
+            big(s_one, b_one, 3, 4).wait_recv()
+        elif i == 3:
+            own_two.wait()
+            big(s_two, b_two, 4, 4).wait_recv()
         for tile in range(8):
-            for o in range(stride):
-                at = pl.ds(8 * stride * tile + o, 8, stride=stride)
-                ref[at, :] = swap_blocks(ref[at, :])
+            for h in range(2):
+                at = pl.ds(8 * stride * ring_tile(tile) + h * (stride // 2) + o, 8, stride=stride)
+                dst[h, :, 128 * tile : 128 * tile + 128] = swap_blocks(ring_order(ref[at, :], tile))
+        store = pltpu.make_async_copy(dst, hbm, out_sem.at[i])
+        store.start()
+        stores.append(store)
 
     all_rows(NT - 1, sums_t, sums_t, 1).wait_recv()
     sums = jnp.sum(fold(sums_t[...]), axis=0, keepdims=True)
@@ -380,18 +416,14 @@
     second = alpha0 * alpha1
     c0, c1 = 1.0 - first + second, first - 2.0 * second
 
-    for tile in range(8):
-        cols = slice(128 * tile, 128 * tile + 128)
-        for h in range(2):
-            z = b_z[pl.ds(16 * tile + h, 8, stride=2), :]
-            n_a = b_one[pl.ds(32 * tile + 2 * h, 8, stride=4), :]
-            s_a = b_one[pl.ds(32 * tile + 2 * h + 1, 8, stride=4), :]
-            n_b = b_two[pl.ds(32 * tile + 2 * h, 8, stride=4), :]
-            s_b = b_two[pl.ds(32 * tile + 2 * h + 1, 8, stride=4), :]
-            x_ref[h, :, cols] = (first - second) * z + second * s_a
-            r_ref[h, :, cols] = c0 * r_ref[h, :, cols] + c1 * n_a + second * n_b
-            p_ref[h, :, cols] = c0 * z + c1 * s_a + second * s_b
-
+    row = iota((8, 128), 0)
+    coef_ref[...] = jnp.where(
+        row == 0,
+        first - second,
+        jnp.where(row == 1, second, jnp.where(row == 2, c0, c1)),
+    )
+    for store in stores:
+        store.wait()
     for copy in copies_0 + copies_1:
         copy.wait_send()
     big(s_mask, b_mask, 0, 2).wait_send()
@@ -403,21 +435,36 @@
     all_rows(NT - 1, sums_t, sums_t, 1).wait_send()
 
 
+def combine(z_ref, na_ref, sa_ref, nb_ref, sb_ref, r_ref, coef_ref, x_out, r_out, p_out):
+    q0, q1, q2, q3 = [coef_ref[i : i + 1, 0:1].reshape(1, 1, 1) for i in range(4)]
+    for tile in range(8):
+        at = (slice(None), slice(None), slice(128 * tile, 128 * tile + 128))
+        z, sa = z_ref[at], sa_ref[at]
+        x_out[at] = q0 * z + q1 * sa
+        r_out[at] = q2 * r_ref[at] + q3 * na_ref[at] + q1 * nb_ref[at]
+        p_out[at] = q2 * z + q3 * sa + q1 * sb_ref[at]
+
+
 def per_device(observations, obs_noise, prior_noise, observed, kappa_sq, obs_precision):
     vmem = pl.BlockSpec(memory_space=pltpu.VMEM)
+    hbm = pl.BlockSpec(memory_space=pl.ANY)
     out = jax.ShapeDtypeStruct(observations.shape, F32)
 
     def buf(*shape):
         return pltpu.VMEM(shape, F32)
 
-    return pl.pallas_call(
+    block = observations.shape
+    parts = pl.pallas_call(
         kernel,
-        out_shape=(out, out, out),
-        in_specs=[vmem] * 6,
-        out_specs=(vmem,) * 3,
+        out_shape=(out,) * 6 + (jax.ShapeDtypeStruct((8, 128), F32),),
+        in_specs=[hbm] * 6,
+        out_specs=(hbm,) * 6 + (vmem,),
         scratch_shapes=[
+            buf(*block), buf(*block), buf(*block), pltpu.VMEM(block, jnp.int32),
+            buf(*kappa_sq.shape), buf(*kappa_sq.shape),
+            buf(*block), buf(*block), buf(*block), buf(*block), buf(*block), buf(*block),
             buf(128, 128), buf(128, 128), buf(128, 128), buf(128, 128),
-            buf(128, 128), buf(128, 128), buf(LEVELS, 128, 128), buf(128, 128),
+            buf(128, 128), buf(LEVELS, 128, 128), buf(128, 128),
             buf(128, 128), buf(128, 128),
             buf(128, 128), buf(256, 128), buf(256, 128),
             buf(128, 128), buf(256, 128), buf(256, 128),
@@ -426,10 +473,14 @@
             pltpu.SemaphoreType.DMA((5,)), pltpu.SemaphoreType.DMA((5,)),
             pltpu.SemaphoreType.DMA((8,)), pltpu.SemaphoreType.DMA((8,)),
             pltpu.SemaphoreType.DMA((2,)), pltpu.SemaphoreType.DMA((2,)),
-            pltpu.SemaphoreType.DMA((5,)),
+            pltpu.SemaphoreType.DMA((5,)), pltpu.SemaphoreType.DMA((6,)),
+            pltpu.SemaphoreType.DMA((6,)),
         ],
         compiler_params=pltpu.CompilerParams(collective_id=0, has_side_effects=True),
     )(observations, obs_noise, prior_noise, observed, kappa_sq, obs_precision)
+    return pl.pallas_call(
+        combine, out_shape=(out, out, out), in_specs=[vmem] * 7, out_specs=(vmem,) * 3
+    )(*parts)
 
 
 def solution(mesh):

time: 55.5 us -> 48 us (0.86)
  Pallas kernels: 51.6 us -> 47.2 us
  local copies, waits for them, and re-layouts: 3 us -> 0 us
    pallas_call x1 -> x2, Pallas kernels: 51.6 us -> 47.2 us  [the longest x1 45.5 us: per_device(): pl.pallas_call(kernel, out_shape=(out,) * 6 + (jax.ShapeDtypeStruct((8, 1...]
    unnamed x7 -> x0, local copies, waits for them, and re-layouts: 3 us -> none
where the time goes in v2:
time: 48 us; the launch traced here: 47.8 us
  Pallas kernels  47.2 us (98%)
  between operations  0.64 us (1%)
    pallas_call x1, Pallas kernels, per_device(): pl.pallas_call(kernel, out_shape=(out,) * 6 + (jax.ShapeDtypeStruct((8, 1...  45.5 us
    pallas_call x1, Pallas kernels, per_device(): pl.pallas_call(combine, out_shape=(out, out, out), in_specs=[vmem] * 7, o...  1.72 us

profile of v2, /device:TPU:1, one launch (start us, length us, event | category | flops | bytes accessed | tf_op | source)
XLA Modules:
  0.0 47.8 jit_solution(13295820895040411949)
XLA Ops:
  0.6 45.5 %shard_map.85 = (f32[2,8,1024]{2,1,0:T(8,128)}, f32[2,8,1024]{2,1,0:T(8,128)}, f32[2,8,1024]{2,1,0:T(8,128)}, f32[2,8,1024]{2,1,0:T(8,128)}, f32[2,8,1024]{2,1,0...) custom-call(f32[2,8,1024]{2,1,0:T(8,128)} %obs_hbm.1, f32[2,8,1024]{2,1,0:T(8,128)} %noise_hbm.1, ...), custom_call_target="tpu_custom_call" | custom-call | tf_op jit(solution)/shard_map/pallas_call | solution.py:457
  46.1 1.7 %shard_map.86 = (f32[2,8,1024]{2,1,0:T(8,128)}, f32[2,8,1024]{2,1,0:T(8,128)}, f32[2,8,1024]{2,1,0:T(8,128)}) custom-call(f32[2,8,1024]{2,1,0:T(8,128)} %get-tuple-element.10.z_ref, f32[2,8,1024]{2,1,0:T(8,128)} %get-tuple-element.11.na_ref, f32[2,8,1024]{2,1,0:T(8,128)} %get-tuple-element.12.sa_ref, f32[2,8,1024]{2,1,0:T(8,128)} %get-tuple-element.13.nb_ref, ...), custom_call_target="tpu_custom_call" | custom-call | tf_op jit(solution)/shard_map/pallas_call | solution.py:481

commit v3 on v2

--- a/solution.py
+++ b/solution.py
@@ -11,7 +11,6 @@
 F32 = jnp.float32
 NT = 64
 NY = 8
-LEVELS = 7
 
 
 def patch_of(m):
@@ -68,7 +67,7 @@
     z_hbm, na_hbm, sa_hbm, nb_hbm, sb_hbm, r_hbm, coef_ref,
     obs_ref, noise_ref, prior_ref, mask_ref, kappa_ref, prec_ref,
     z_all, na_all, sa_all, nb_all, sb_all, r_all,
-    s_mask, s_right, b_mask, b_right, stencil, gain, last, rc, nc,
+    s_mask, s_right, b_mask, b_right, down, joins, nc,
     s_z, s_one, s_two, b_z, b_one, b_two, pads, cols_out, side_in, rows_in,
     sums_y, sums_t, mine, one_row,
     send_big, recv_big, halo_send, halo_recv, sum_send, sum_recv, own_sem, in_sem, out_sem,
@@ -92,11 +91,6 @@
 
     def greet(t):
         pl.semaphore_signal(barrier, inc=1, device_id={"tm": t}, device_id_type=MESH)
-
-    each_peer(greet)
-    for k in range(1, NY):
-        t = lax.rem(y + k, NY)
-        pl.semaphore_signal(barrier, inc=1, device_id={"rows": t}, device_id_type=MESH)
 
     loads = [
         pltpu.make_async_copy(src, dst, in_sem.at[i])
@@ -113,6 +107,11 @@
     ]
     for load in loads:
         load.start()
+
+    each_peer(greet)
+    for k in range(1, NY):
+        t = lax.rem(y + k, NY)
+        pl.semaphore_signal(barrier, inc=1, device_id={"rows": t}, device_id_type=MESH)
     for load in loads:
         load.wait()
 
@@ -164,19 +163,11 @@
     own_right = to_all(s_right, b_right, 1, 2)
 
     tile, back = j // 8, j % 8
-    shift = lax.rem(128 - 16 * back, 128)
     columns = pl.ds(pl.multiple_of(tile * 128, 128), 128)
-
-    def per_cell(ref):
-        rows = pltpu.roll(ref[:, columns], shift, 1)
-        turned = jnp.concatenate([rows, jnp.zeros((120, 128), F32)], axis=0).T
-        return [jnp.broadcast_to(turned[0:16, r : r + 1], (16, 128)) for r in range(8)]
-
-    kappa = per_cell(kappa_ref)
-    for r in range(8):
-        stencil[pl.ds(16 * r, 16), :] = 1.0 / (kappa[r] + 4.0)
-    one_row[...] = swap_blocks(prec_ref[:, columns] / (kappa_ref[:, columns] + 4.0))
-    ratio = one_row[pl.ds(back, 1), :]
+    one_row[...] = swap_blocks(1.0 / (kappa_ref[:, columns] + 4.0))
+    per_stencil = jnp.broadcast_to(one_row[pl.ds(back, 1), :], (8, 128))
+    mine[...] = swap_blocks(prec_ref[:, columns])
+    ratio = per_stencil * mine[pl.ds(back, 1), :]
 
     own_mask.wait()
     big(s_mask, b_mask, 0, 2).wait_recv()
@@ -202,32 +193,53 @@
         ]
     b = jnp.where(seg == 0, 0.0, pltpu.roll(b, 1, 0))
     d = jnp.where(seg == 0, 1.0, pltpu.roll(d, 1, 0))
+    inverses = []
     for k in range(16):
         before_b, before_d = b, d
         bd = b + d
         b, d = w[k] * bd + RHO_SQ * b, bd
-        pivot = (b + d) / d
+        inverse = d / (b + d)
         if k == 15:
             before = before_b / before_d
             final = w[k] + ((1.0 - RHO_SQ) + before) / (1.0 + before)
-            pivot = jnp.where(seg == 7, final, pivot)
-        rc[pl.ds(k, 8, stride=16), :] = 1.0 / pivot
-    inverse = rc[...].T
-    last[...] = inverse
-    g = pltpu.roll(jnp.where(iota((128, 128), 1) == 127, 0.0, RHO * inverse), 1, 1)
-    for k in range(LEVELS):
-        gain[k] = g
-        if k < LEVELS - 1:
-            g = g * pltpu.roll(g, 1 << k, 1)
-
-    def solve(v):
-        v = v * stencil[...]
-        for k in range(LEVELS):
-            v = v + gain[k] * pltpu.roll(v, 1 << k, 1)
-        v = v * last[...]
-        for k in range(LEVELS):
-            v = v + pltpu.roll(gain[k] * v, 128 - (1 << k), 1)
-        return v
+            inverse = jnp.where(seg == 7, 1.0 / final, inverse)
+        inverses.append(inverse)
+    carry = [RHO * inverse for inverse in inverses]
+    carry[15] = jnp.where(seg == 7, 0.0, carry[15])
+    into = pltpu.roll(carry[15], 1, 0)
+    for k in range(16):
+        down[0, k], down[1, k], down[2, k] = inverses[k], carry[k], into
+        if k < 15:
+            into = into * carry[k]
+    back_in = carry[15]
+    for k in range(15, -1, -1):
+        down[3, k] = back_in
+        if k > 0:
+            back_in = back_in * carry[k - 1]
+    for i, n in enumerate((1, 2, 4)):
+        joins[i], joins[3 + i] = into, back_in
+        into, back_in = into * pltpu.roll(into, n, 0), back_in * pltpu.roll(back_in, 8 - n, 0)
+
+    def solve(load, keep):
+        y, values = None, []
+        for k in range(16):
+            f = load(k) * per_stencil
+            y = f if k == 0 else f + down[1, k - 1] * y
+            values.append(y)
+        for i, n in enumerate((1, 2, 4)):
+            y = y + joins[i] * pltpu.roll(y, n, 0)
+        y = pltpu.roll(y, 1, 0)
+        values = [(v + down[2, k] * y) * down[0, k] for k, v in enumerate(values)]
+        for k in range(14, -1, -1):
+            values[k] = values[k] + down[1, k] * values[k + 1]
+        z = values[0]
+        for i, n in enumerate((1, 2, 4)):
+            z = z + joins[3 + i] * pltpu.roll(z, 8 - n, 0)
+        z = pltpu.roll(z, 7, 0)
+        for k in range(16):
+            values[k] = values[k] + down[3, k] * z
+            keep(k, values[k])
+        return values
 
     left, right_dev = device_of(lax.rem(j + NT - 1, NT)), device_of(lax.rem(j + 1, NT))
     above, below = lax.rem(y + NY - 1, NY), lax.rem(y + 1, NY)
@@ -291,25 +303,37 @@
 
     own_right.wait()
     big(s_right, b_right, 1, 2).wait_recv()
-    rc[...] = b_right[...].T
-    z0 = solve(rc[...])
-    copies_0 = halo_start(0, z0)
-    s_z[...] = z0.T
+    def right_at(k):
+        return b_right[pl.ds(k, 8, stride=16), :]
+
+    def keep_z(k, v):
+        s_z[pl.ds(k, 8, stride=16), :] = v
+
+    def total_of(load, values):
+        return sum(load(k) * v for k, v in enumerate(values))
+
+    z_values = solve(right_at, keep_z)
+    copies_0 = halo_start(0, s_z[...].T)
+    rz_part = total_of(right_at, z_values)
+
+    def pair(ref, n):
+        ref[pl.ds(0, 128, stride=2), :] = n.T
+
+        def load(k):
+            return ref[pl.ds(2 * k, 8, stride=32), :]
+
+        def keep(k, v):
+            ref[pl.ds(2 * k + 1, 8, stride=32), :] = v
+
+        return load, solve(load, keep)
+
+    n0 = neighbours(0, copies_0)
+    load_0, s_values = pair(s_one, n0)
+    copies_1 = halo_start(1, s_one[pl.ds(1, 128, stride=2), :].T)
     own_z = to_all(s_z, b_z, 2, 2)
-    rz_part = fold(rc[...] * z0)
-
-    n0 = neighbours(0, copies_0)
-    s0 = solve(n0)
-    copies_1 = halo_start(1, s0)
-
-    def interleave(ref, even, odd):
-        ref[pl.ds(0, 128, stride=2), :] = even.T
-        ref[pl.ds(1, 128, stride=2), :] = odd.T
-
-    interleave(s_one, n0, s0)
     own_one = to_all(s_one, b_one, 3, 4)
-    e1_part = fold(rc[...] * s0)
-    e2_part = fold(n0 * s0)
+    e1_part = total_of(right_at, s_values)
+    e2_part = total_of(load_0, s_values)
 
     n1 = neighbours(1, copies_1)
     e3_part = fold(n1 * jnp.concatenate([pads[1, pl.ds(32 * r + 8, 16), :] for r in range(8)], axis=0))
@@ -318,27 +342,25 @@
     total = jnp.zeros((8, 128), F32)
     for i, part in enumerate((rz_part, e1_part, e2_part, e3_part)):
         total = jnp.where(sub == i, jnp.sum(part, axis=0, keepdims=True), total)
-    mine[...] = total
-    sums_y[pl.ds(pl.multiple_of(8 * y, 8), 8), :] = total
-
-    def rows_copy(t):
-        return pltpu.make_async_remote_copy(
-            src_ref=mine,
-            dst_ref=sums_y.at[pl.ds(pl.multiple_of(8 * y, 8), 8)],
-            send_sem=sum_send.at[0],
-            recv_sem=sum_recv.at[0],
-            device_id={"rows": t},
+    total = total + pltpu.roll(total, 64, 1)
+    total = total + pltpu.roll(total, 32, 1)
+    total = jnp.where(iota((8, 128), 1) // 32 == sub, total, 0.0)
+    one_row[...] = jnp.broadcast_to(jnp.sum(total, axis=0, keepdims=True), (8, 128))
+    sums_t[pl.ds(me, 1), :] = one_row[0:1, :]
+
+    def send_sum(t):
+        pltpu.make_async_remote_copy(
+            src_ref=one_row.at[pl.ds(0, 1)],
+            dst_ref=sums_t.at[pl.ds(me, 1)],
+            send_sem=sum_send.at[1],
+            recv_sem=sum_recv.at[1],
+            device_id={"tm": t},
             device_id_type=MESH,
-        )
-
-    def send_rows(k, carry):
-        rows_copy(lax.rem(y + k, NY)).start()
-        return carry
-
-    lax.fori_loop(1, NY, send_rows, 0)
-
-    s1 = solve(n1)
-    interleave(s_two, n1, s1)
+        ).start()
+
+    each_peer(send_sum)
+
+    pair(s_two, n1)
     own_two = to_all(s_two, b_two, 4, 4)
 
     def all_rows(n, src, dst, slot):
@@ -351,27 +373,18 @@
             device_id_type=MESH,
         )
 
-    all_rows(8 * (NY - 1), sums_y, sums_y, 0).wait_recv()
-    part = fold(sums_y[...])
-    part = part + pltpu.roll(part, 64, 1)
-    part = part + pltpu.roll(part, 32, 1)
-    part = jnp.where(iota((8, 128), 1) // 32 == sub, part, 0.0)
-    one_row[...] = jnp.broadcast_to(jnp.sum(part, axis=0, keepdims=True), (8, 128))
-    sums_t[pl.ds(me, 1), :] = one_row[0:1, :]
-
-    def send_sums(i, carry):
-        t = lax.rem(me + 1 + lax.rem(i + 23, NT - 1), NT)
+    all_rows(NT - 1, sums_t, sums_t, 1).wait_recv()
+    mine[...] = fold(sums_t[...])
+    sums_y[pl.ds(pl.multiple_of(8 * y, 8), 8), :] = mine[...]
+    for k in range(1, NY):
         pltpu.make_async_remote_copy(
-            src_ref=one_row.at[pl.ds(0, 1)],
-            dst_ref=sums_t.at[pl.ds(me, 1)],
-            send_sem=sum_send.at[1],
-            recv_sem=sum_recv.at[1],
-            device_id={"tm": t},
+            src_ref=mine,
+            dst_ref=sums_y.at[pl.ds(pl.multiple_of(8 * y, 8), 8)],
+            send_sem=sum_send.at[0],
+            recv_sem=sum_recv.at[0],
+            device_id={"rows": lax.rem(y + k, NY)},
             device_id_type=MESH,
         ).start()
-        return carry
-
-    lax.fori_loop(0, NT - 1, send_sums, 0)
 
     stores = []
     store = pltpu.make_async_copy(r_all, r_hbm, out_sem.at[5])
@@ -402,8 +415,8 @@
         store.start()
         stores.append(store)
 
-    all_rows(NT - 1, sums_t, sums_t, 1).wait_recv()
-    sums = jnp.sum(fold(sums_t[...]), axis=0, keepdims=True)
+    all_rows(8 * (NY - 1), sums_y, sums_y, 0).wait_recv()
+    sums = jnp.sum(fold(sums_y[...]), axis=0, keepdims=True)
     group = iota((1, 128), 1) // 32
     rz0, e1, e2, e3 = [lane_sum(jnp.where(group == i, sums, 0.0)) for i in range(4)]
     curved = rz0 - e1
@@ -464,8 +477,7 @@
             buf(*kappa_sq.shape), buf(*kappa_sq.shape),
             buf(*block), buf(*block), buf(*block), buf(*block), buf(*block), buf(*block),
             buf(128, 128), buf(128, 128), buf(128, 128), buf(128, 128),
-            buf(128, 128), buf(LEVELS, 128, 128), buf(128, 128),
-            buf(128, 128), buf(128, 128),
+            buf(4, 16, 8, 128), buf(6, 8, 128), buf(128, 128),
             buf(128, 128), buf(256, 128), buf(256, 128),
             buf(128, 128), buf(256, 128), buf(256, 128),
             buf(2, 256, 128), buf(2, 2, 8, 128), buf(2, 2, 8, 128), buf(2, 2, 16, 128),

time: 48 us -> 45.6 us (0.950)
  Pallas kernels: 47.2 us -> 44.7 us
    pallas_call x1, Pallas kernels: 45.5 us -> 43 us  [per_device(): pl.pallas_call(kernel, out_shape=(out,) * 6 + (jax.ShapeDtypeStruct((8, 1...]
where the time goes in v3:
time: 45.6 us; the launch traced here: 45.3 us
  Pallas kernels  44.7 us (98%)
  between operations  0.64 us (1%)
    pallas_call x1, Pallas kernels, per_device(): pl.pallas_call(kernel, out_shape=(out,) * 6 + (jax.ShapeDtypeStruct((8, 1...  43 us
    pallas_call x1, Pallas kernels, per_device(): pl.pallas_call(combine, out_shape=(out, out, out), in_specs=[vmem] * 7, o...  1.72 us

profile of v3, /device:TPU:1, one launch (start us, length us, event | category | flops | bytes accessed | tf_op | source)
XLA Modules:
  0.0 45.3 jit_solution(2075771330846255947)
XLA Ops:
  0.6 43.0 %shard_map.85 = (f32[2,8,1024]{2,1,0:T(8,128)}, f32[2,8,1024]{2,1,0:T(8,128)}, f32[2,8,1024]{2,1,0:T(8,128)}, f32[2,8,1024]{2,1,0:T(8,128)}, f32[2,8,1024]{2,1,0...) custom-call(f32[2,8,1024]{2,1,0:T(8,128)} %obs_hbm.1, f32[2,8,1024]{2,1,0:T(8,128)} %noise_hbm.1, ...), custom_call_target="tpu_custom_call" | custom-call | tf_op jit(solution)/shard_map/pallas_call | solution.py:470
  43.6 1.7 %shard_map.86 = (f32[2,8,1024]{2,1,0:T(8,128)}, f32[2,8,1024]{2,1,0:T(8,128)}, f32[2,8,1024]{2,1,0:T(8,128)}) custom-call(f32[2,8,1024]{2,1,0:T(8,128)} %get-tuple-element.10.z_ref, f32[2,8,1024]{2,1,0:T(8,128)} %get-tuple-element.11.na_ref, f32[2,8,1024]{2,1,0:T(8,128)} %get-tuple-element.12.sa_ref, f32[2,8,1024]{2,1,0:T(8,128)} %get-tuple-element.13.nb_ref, ...), custom_call_target="tpu_custom_call" | custom-call | tf_op jit(solution)/shard_map/pallas_call | solution.py:493

commit v4 on v3

--- a/solution.py
+++ b/solution.py
@@ -64,13 +64,12 @@
 
 def kernel(
     obs_hbm, noise_hbm, prior_hbm, mask_hbm, kappa_hbm, prec_hbm,
-    z_hbm, na_hbm, sa_hbm, nb_hbm, sb_hbm, r_hbm, coef_ref,
+    z_all, na_all, sa_all, nb_all, sb_all, r_all, coef_ref,
     obs_ref, noise_ref, prior_ref, mask_ref, kappa_ref, prec_ref,
-    z_all, na_all, sa_all, nb_all, sb_all, r_all,
     s_mask, s_right, b_mask, b_right, down, joins, nc,
     s_z, s_one, s_two, b_z, b_one, b_two, pads, cols_out, side_in, rows_in,
     sums_y, sums_t, mine, one_row,
-    send_big, recv_big, halo_send, halo_recv, sum_send, sum_recv, own_sem, in_sem, out_sem,
+    send_big, recv_big, halo_send, halo_recv, sum_send, sum_recv, own_sem, in_sem,
 ):
     me, y = lax.axis_index("tm"), lax.axis_index("rows")
     j = patch_of(me)
@@ -386,18 +385,14 @@
             device_id_type=MESH,
         ).start()
 
-    stores = []
-    store = pltpu.make_async_copy(r_all, r_hbm, out_sem.at[5])
-    store.start()
-    stores.append(store)
     outs = (
-        (0, b_z, 2, 0, z_all, z_hbm),
-        (1, b_one, 4, 0, na_all, na_hbm),
-        (2, b_one, 4, 1, sa_all, sa_hbm),
-        (3, b_two, 4, 0, nb_all, nb_hbm),
-        (4, b_two, 4, 1, sb_all, sb_hbm),
+        (0, b_z, 2, 0, z_all),
+        (1, b_one, 4, 0, na_all),
+        (2, b_one, 4, 1, sa_all),
+        (3, b_two, 4, 0, nb_all),
+        (4, b_two, 4, 1, sb_all),
     )
-    for i, ref, stride, o, dst, hbm in outs:
+    for i, ref, stride, o, dst in outs:
         if i == 0:
             own_z.wait()
             big(s_z, b_z, 2, 2).wait_recv()
@@ -411,9 +406,6 @@
             for h in range(2):
                 at = pl.ds(8 * stride * ring_tile(tile) + h * (stride // 2) + o, 8, stride=stride)
                 dst[h, :, 128 * tile : 128 * tile + 128] = swap_blocks(ring_order(ref[at, :], tile))
-        store = pltpu.make_async_copy(dst, hbm, out_sem.at[i])
-        store.start()
-        stores.append(store)
 
     all_rows(8 * (NY - 1), sums_y, sums_y, 0).wait_recv()
     sums = jnp.sum(fold(sums_y[...]), axis=0, keepdims=True)
@@ -435,8 +427,6 @@
         first - second,
         jnp.where(row == 1, second, jnp.where(row == 2, c0, c1)),
     )
-    for store in stores:
-        store.wait()
     for copy in copies_0 + copies_1:
         copy.wait_send()
     big(s_mask, b_mask, 0, 2).wait_send()
@@ -469,13 +459,12 @@
     block = observations.shape
     parts = pl.pallas_call(
         kernel,
-        out_shape=(out,) * 6 + (jax.ShapeDtypeStruct((8, 128), F32),),
+        out_shape=(buf(*block),) * 6 + (buf(8, 128),),
         in_specs=[hbm] * 6,
-        out_specs=(hbm,) * 6 + (vmem,),
+        out_specs=(vmem,) * 7,
         scratch_shapes=[
             buf(*block), buf(*block), buf(*block), pltpu.VMEM(block, jnp.int32),
             buf(*kappa_sq.shape), buf(*kappa_sq.shape),
-            buf(*block), buf(*block), buf(*block), buf(*block), buf(*block), buf(*block),
             buf(128, 128), buf(128, 128), buf(128, 128), buf(128, 128),
             buf(4, 16, 8, 128), buf(6, 8, 128), buf(128, 128),
             buf(128, 128), buf(256, 128), buf(256, 128),
@@ -486,13 +475,12 @@
             pltpu.SemaphoreType.DMA((8,)), pltpu.SemaphoreType.DMA((8,)),
             pltpu.SemaphoreType.DMA((2,)), pltpu.SemaphoreType.DMA((2,)),
             pltpu.SemaphoreType.DMA((5,)), pltpu.SemaphoreType.DMA((6,)),
-            pltpu.SemaphoreType.DMA((6,)),
         ],
         compiler_params=pltpu.CompilerParams(collective_id=0, has_side_effects=True),
     )(observations, obs_noise, prior_noise, observed, kappa_sq, obs_precision)
     return pl.pallas_call(
         combine, out_shape=(out, out, out), in_specs=[vmem] * 7, out_specs=(vmem,) * 3
-    )(*parts)
+    )(*[pltpu.with_memory_space_constraint(part, pltpu.VMEM) for part in parts])
 
 
 def solution(mesh):

time: 45.6 us -> 43.9 us (0.963)
  Pallas kernels: 44.7 us -> 43.1 us
    pallas_call x1, Pallas kernels: 1.72 us -> 0.72 us  [per_device(): pl.pallas_call(combine, out_shape=(out, out, out), in_specs=[vmem] * 7, o...]
    pallas_call x1, Pallas kernels: 43 us -> 42.3 us  [per_device(): pl.pallas_call(kernel, out_shape=(buf(*block),) * 6 + (buf(8, 128),), in_...]
where the time goes in v4:
time: 43.9 us; the launch traced here: 43.7 us
  Pallas kernels  43.1 us (98%)
  between operations  0.64 us (1%)
    pallas_call x1, Pallas kernels, per_device(): pl.pallas_call(kernel, out_shape=(buf(*block),) * 6 + (buf(8, 128),), in_...  42.3 us

profile of v4, /device:TPU:1, one launch (start us, length us, event | category | flops | bytes accessed | tf_op | source)
XLA Modules:
  0.0 43.7 jit_solution(9840592966001612421)
XLA Ops:
  0.6 42.3 %shard_map.85 = (f32[2,8,1024]{2,1,0:T(8,128)S(1)}, f32[2,8,1024]{2,1,0:T(8,128)S(1)}, f32[2,8,1024]{2,1,0:T(8,128)S(1)}, f32[2,8,1024]{2,1,0:T(8,128)S(1)}, f32...) custom-call(f32[2,8,1024]{2,1,0:T(8,128)} %obs_hbm.1, f32[2,8,1024]{2,1,0:T(8,128)} %noise_hbm.1, ...), custom_call_target="tpu_custom_call" | custom-call | tf_op jit(solution)/shard_map/pallas_call | solution.py:460
  43.0 0.7 %shard_map.86 = (f32[2,8,1024]{2,1,0:T(8,128)}, f32[2,8,1024]{2,1,0:T(8,128)}, f32[2,8,1024]{2,1,0:T(8,128)}) custom-call(f32[2,8,1024]{2,1,0:T(8,128)S(1)} %get-tuple-element.10.z_ref, f32[2,8,1024]{2,1,0:T(8,128)S(1)} %get-tuple-element.11.na_ref, f32[2,8,1024]{2,1,0:T(8,128)S(1)} %get-tuple-element.12.sa_ref, f32[2,8,1024]{2,1,0:T(8,128)S(1)} %get-tuple-element.13.nb_ref, ...), custom_call_target="tpu_custom_call" | custom-call | tf_op jit(solution)/shard_map/pallas_call | solution.py:481

commit v5 on v4

--- a/solution.py
+++ b/solution.py
@@ -11,6 +11,14 @@
 F32 = jnp.float32
 NT = 64
 NY = 8
+
+
+def hops(o):
+    z, x = (o // 2) % 8, o // 16
+    return min(z, 8 - z) + min(x, 4 - x)
+
+
+FAR_FIRST = sorted(range(1, NT), key=lambda o: (-hops(o), o))
 
 
 def patch_of(m):
@@ -77,16 +85,9 @@
     barrier = pltpu.get_barrier_semaphore()
 
     def each_peer(act):
-        def block(b, carry):
-            base = me + 22 + 7 * b + jnp.where(b >= 6, 1, 0)
-            base = base - jnp.where(base >= NT, NT, 0)
-            base = base - jnp.where(base >= NT, NT, 0)
-            for i in range(7):
-                t = base + i
-                act(t - jnp.where(t >= NT, NT, 0))
-            return carry
-
-        lax.fori_loop(0, 9, block, 0)
+        for o in FAR_FIRST:
+            t = me + o
+            act(t - jnp.where(t >= NT, NT, 0))
 
     def greet(t):
         pl.semaphore_signal(barrier, inc=1, device_id={"tm": t}, device_id_type=MESH)
@@ -108,7 +109,7 @@
         load.start()
 
     each_peer(greet)
-    for k in range(1, NY):
+    for k in (4, 3, 5, 2, 6, 1, 7):
         t = lax.rem(y + k, NY)
         pl.semaphore_signal(barrier, inc=1, device_id={"rows": t}, device_id_type=MESH)
     for load in loads:
@@ -375,7 +376,7 @@
     all_rows(NT - 1, sums_t, sums_t, 1).wait_recv()
     mine[...] = fold(sums_t[...])
     sums_y[pl.ds(pl.multiple_of(8 * y, 8), 8), :] = mine[...]
-    for k in range(1, NY):
+    for k in (4, 3, 5, 2, 6, 1, 7):
         pltpu.make_async_remote_copy(
             src_ref=mine,
             dst_ref=sums_y.at[pl.ds(pl.multiple_of(8 * y, 8), 8)],

time: 43.9 us -> 43.2 us (0.984)
  Pallas kernels: 43.1 us -> 42.4 us
    pallas_call x1, Pallas kernels: 42.3 us -> 41.6 us  [per_device(): pl.pallas_call(kernel, out_shape=(buf(*block),) * 6 + (buf(8, 128),), in_...]
where the time goes in v5:
time: 43.2 us; the launch traced here: 43 us
  Pallas kernels  42.4 us (98%)
  between operations  0.64 us (1%)
    pallas_call x1, Pallas kernels, per_device(): pl.pallas_call(kernel, out_shape=(buf(*block),) * 6 + (buf(8, 128),), in_...  41.6 us

profile of v5, /device:TPU:1, one launch (start us, length us, event | category | flops | bytes accessed | tf_op | source)
XLA Modules:
  0.0 43.0 jit_solution(1317604890671248212)
XLA Ops:
  0.6 41.6 %shard_map.85 = (f32[2,8,1024]{2,1,0:T(8,128)S(1)}, f32[2,8,1024]{2,1,0:T(8,128)S(1)}, f32[2,8,1024]{2,1,0:T(8,128)S(1)}, f32[2,8,1024]{2,1,0:T(8,128)S(1)}, f32...) custom-call(f32[2,8,1024]{2,1,0:T(8,128)} %obs_hbm.1, f32[2,8,1024]{2,1,0:T(8,128)} %noise_hbm.1, ...), custom_call_target="tpu_custom_call" | custom-call | tf_op jit(solution)/shard_map/pallas_call | solution.py:461
  42.3 0.7 %shard_map.86 = (f32[2,8,1024]{2,1,0:T(8,128)}, f32[2,8,1024]{2,1,0:T(8,128)}, f32[2,8,1024]{2,1,0:T(8,128)}) custom-call(f32[2,8,1024]{2,1,0:T(8,128)S(1)} %get-tuple-element.10.z_ref, f32[2,8,1024]{2,1,0:T(8,128)S(1)} %get-tuple-element.11.na_ref, f32[2,8,1024]{2,1,0:T(8,128)S(1)} %get-tuple-element.12.sa_ref, f32[2,8,1024]{2,1,0:T(8,128)S(1)} %get-tuple-element.13.nb_ref, ...), custom_call_target="tpu_custom_call" | custom-call | tf_op jit(solution)/shard_map/pallas_call | solution.py:482

commit v6 on v5

--- a/solution.py
+++ b/solution.py
@@ -315,6 +315,7 @@
     z_values = solve(right_at, keep_z)
     copies_0 = halo_start(0, s_z[...].T)
     rz_part = total_of(right_at, z_values)
+    own_z = to_all(s_z, b_z, 2, 2)
 
     def pair(ref, n):
         ref[pl.ds(0, 128, stride=2), :] = n.T
@@ -330,7 +331,6 @@
     n0 = neighbours(0, copies_0)
     load_0, s_values = pair(s_one, n0)
     copies_1 = halo_start(1, s_one[pl.ds(1, 128, stride=2), :].T)
-    own_z = to_all(s_z, b_z, 2, 2)
     own_one = to_all(s_one, b_one, 3, 4)
     e1_part = total_of(right_at, s_values)
     e2_part = total_of(load_0, s_values)

time: 43.2 us -> 42.8 us (level)
  no operation moved by 1% of the time
where the time goes in v6:
time: 42.8 us; the launch traced here: 42.6 us
  Pallas kernels  42 us (98%)
  between operations  0.64 us (1%)
    pallas_call x1, Pallas kernels, per_device(): pl.pallas_call(kernel, out_shape=(buf(*block),) * 6 + (buf(8, 128),), in_...  41.2 us

profile of v6, /device:TPU:1, one launch (start us, length us, event | category | flops | bytes accessed | tf_op | source)
XLA Modules:
  0.0 42.6 jit_solution(2047425076401258663)
XLA Ops:
  0.6 41.2 %shard_map.85 = (f32[2,8,1024]{2,1,0:T(8,128)S(1)}, f32[2,8,1024]{2,1,0:T(8,128)S(1)}, f32[2,8,1024]{2,1,0:T(8,128)S(1)}, f32[2,8,1024]{2,1,0:T(8,128)S(1)}, f32...) custom-call(f32[2,8,1024]{2,1,0:T(8,128)} %obs_hbm.1, f32[2,8,1024]{2,1,0:T(8,128)} %noise_hbm.1, ...), custom_call_target="tpu_custom_call" | custom-call | tf_op jit(solution)/shard_map/pallas_call | solution.py:461
  41.9 0.7 %shard_map.86 = (f32[2,8,1024]{2,1,0:T(8,128)}, f32[2,8,1024]{2,1,0:T(8,128)}, f32[2,8,1024]{2,1,0:T(8,128)}) custom-call(f32[2,8,1024]{2,1,0:T(8,128)S(1)} %get-tuple-element.10.z_ref, f32[2,8,1024]{2,1,0:T(8,128)S(1)} %get-tuple-element.11.na_ref, f32[2,8,1024]{2,1,0:T(8,128)S(1)} %get-tuple-element.12.sa_ref, f32[2,8,1024]{2,1,0:T(8,128)S(1)} %get-tuple-element.13.nb_ref, ...), custom_call_target="tpu_custom_call" | custom-call | tf_op jit(solution)/shard_map/pallas_call | solution.py:482
